TPU v7x, 512 devices: a whole 4x8x8 slice. The times are simulated.
512 devices in a mesh: dp: 8 (over z), expert: 8 (over y_hi, core), etp: 8 (over x, y_lo).
Axes of the slice: x: 4, y: 8 (y_hi: 4, y_lo: 2; y = y_hi * 2 + y_lo), z: 8, core: 2. Of those that a mesh axis runs over, the one named last changes fastest.
Arguments:
- grad_out: bfloat16 [8192, 3072], P(('dp', 'expert'), 'etp'), may hold values from -6 to 6
- routing: int32 [8192, 2], P(('dp', 'expert')), may hold values from 0 to 7, all different within a row; in each aligned block of 128 rows (0 to 127, 128 to 255, ...) at most 48 rows name the same one
- mix_weights: bfloat16 [8192, 2], P(('dp', 'expert')), may hold values from 0.099609375 to 1
- gate_pre: bfloat16 [8, 8, 8, 48, 8192], P('dp', 'expert', None, None, 'etp'), may hold values from -4 to 4
- up_pre: bfloat16 [8, 8, 8, 48, 8192], P('dp', 'expert', None, None, 'etp'), may hold values from -4 to 4
- down_weight: bfloat16 [8, 8192, 3072], P('expert', 'etp', 'dp'), may hold values from -0.0625 to 0.0625
Outputs:
- grad_gate: bfloat16 [8, 8, 8, 48, 8192], P('dp', 'expert', None, None, 'etp')
- grad_up: bfloat16 [8, 8, 8, 48, 8192], P('dp', 'expert', None, None, 'etp')
- grad_mix: float32 [8192, 2], P(('dp', 'expert'))
- grad_down: bfloat16 [8, 8192, 3072], P('expert', 'etp', 'dp')
Inputs may be any that keep to these rules, and one draw needn't show every extreme that they name: `routing`: the two experts of a token differ. Within the tokens of one device (aligned blocks of 128 rows) no expert is named more than 48 times, a bound that some block reaches; every expert is named somewhere.
All inputs are finite; a program needn't handle non-finite values.
Results may differ from a plain program's by a relative error of at most 0.0064.
Values may be sent and summed in bfloat16 or wider, within the bound.
A program may use at most 64 MiB of HBM per device.

v0:
```python
import jax
import jax.numpy as jnp
from jax import lax
from jax.sharding import PartitionSpec as P


def slot_targets(chosen, experts, capacity):
    flattened = chosen.reshape(-1)
    one_hot = (flattened[:, None] == jnp.arange(experts, dtype=jnp.int32)[None, :]).astype(
        jnp.int32
    )
    earlier = jnp.cumsum(one_hot, axis=0) - one_hot
    position = jnp.sum(earlier * one_hot, axis=1)
    return flattened * capacity + position


def swiglu_back(upstream, mix_rows, gate_act, up_act):
    gate_val = gate_act.astype(jnp.float32)
    up_val = up_act.astype(jnp.float32)
    sigmoid_a = jax.nn.sigmoid(gate_val)
    silu_a = gate_val * sigmoid_a
    hidden = silu_a * up_val
    scaled = mix_rows.astype(jnp.float32)[:, None] * upstream
    grad_gate = (scaled * up_val * sigmoid_a * (1.0 + gate_val * (1.0 - sigmoid_a))).astype(
        jnp.bfloat16
    )
    grad_up = (scaled * silu_a).astype(jnp.bfloat16)
    row_terms = jnp.sum(upstream * hidden, axis=1)
    return (grad_gate, grad_up, row_terms, hidden.astype(jnp.bfloat16))


def per_device(grad_out, routing, mix_weights, gate_pre, up_pre, down_weight):
    experts = lax.axis_size("expert")
    replicas = lax.axis_size("dp")
    capacity = gate_pre.shape[3]
    hidden_here = gate_pre.shape[4]
    slot_count = experts * capacity
    tokens_here = routing.shape[0]
    targets = slot_targets(routing, experts, capacity)
    send_mix = (
        jnp.zeros((slot_count,), jnp.bfloat16)
        .at[targets]
        .set(mix_weights.reshape(-1))
        .reshape(experts, capacity)
    )
    send_rows = (
        jnp.zeros((slot_count, grad_out.shape[1]), jnp.bfloat16)
        .at[targets]
        .set(jnp.repeat(grad_out, 2, axis=0))
    )
    routed, routed_mix = (
        lax.all_to_all(
            send_rows.reshape(experts, capacity, -1),
            "expert",
            split_axis=0,
            concat_axis=0,
            tiled=True,
        ),
        lax.all_to_all(send_mix, "expert", split_axis=0, concat_axis=0, tiled=True),
    )
    routed = lax.all_gather(routed.reshape(slot_count, -1), "etp", axis=1, tiled=True)
    routed_mix = routed_mix.reshape(slot_count)
    weight = down_weight[0]
    upstream = lax.dot_general(
        routed,
        lax.all_gather(weight, "dp", axis=1, tiled=True),
        (((1,), (1,)), ((), ())),
        preferred_element_type=jnp.float32,
    )
    grad_gate, grad_up, row_terms, hidden_rounded = swiglu_back(
        upstream,
        routed_mix,
        gate_pre.reshape(slot_count, hidden_here),
        up_pre.reshape(slot_count, hidden_here),
    )
    row_terms = lax.psum(row_terms, "etp")
    returned = lax.all_to_all(
        row_terms.reshape(experts, capacity), "expert", split_axis=0, concat_axis=0, tiled=True
    )
    grad_mix = returned.reshape(-1)[targets].reshape(tokens_here, 2)
    weighted = (routed_mix.astype(jnp.float32)[:, None] * routed.astype(jnp.float32)).astype(
        jnp.bfloat16
    )
    width_here = weight.shape[1]
    partial_value = lax.dot_general(
        hidden_rounded, weighted, (((0,), (0,)), ((), ())), preferred_element_type=jnp.float32
    ).astype(jnp.bfloat16)
    blocks = lax.all_to_all(partial_value, "dp", split_axis=1, concat_axis=0, tiled=True)
    grad_down = jnp.sum(
        blocks.reshape(replicas, hidden_here, width_here).astype(jnp.float32), axis=0
    )
    shape_out = (1, 1, experts, capacity, hidden_here)
    return (
        grad_gate.reshape(shape_out),
        grad_up.reshape(shape_out),
        grad_mix,
        grad_down.astype(jnp.bfloat16)[None],
    )


def solution(mesh):
    in_specs = (
        P(("dp", "expert"), "etp"),
        P(("dp", "expert"), None),
        P(("dp", "expert"), None),
        P("dp", "expert", None, None, "etp"),
        P("dp", "expert", None, None, "etp"),
        P("expert", "etp", "dp"),
    )
    out_specs = (
        P("dp", "expert", None, None, "etp"),
        P("dp", "expert", None, None, "etp"),
        P(("dp", "expert"), None),
        P("expert", "etp", "dp"),
    )
    return jax.shard_map(
        per_device, mesh=mesh, in_specs=in_specs, out_specs=out_specs, check_vma=False
    )
```

profile of v0, /device:TPU:1, one launch (start us, length us, event | category | flops | bytes accessed | tf_op | source)
XLA Modules:
  0.0 378.1 jit_solution(7718738736647603038)
XLA Ops:
  7.2 0.7 broadcast_multiply_fusion
  7.9 0.9 copy.16
  9.3 0.6 reduce-window.6
  9.9 0.2 slice_reduce_fusion
  10.2 1.0 broadcast_in_dim.20
  11.3 1.6 scatter_custom_fusion.1
  12.9 21.3 %all_to_all.37 = bf16[8,48,384]{2,1,0:T(8,128)(2,1)} all-to-all(bf16[8,48,384]{2,1,0:T(8,128)(2,1)S(1)} %bitcast.42), channel_id=1, replica_groups=mesh['dp'=8,'expert'=8,'etp'=8] {'expert'}, dimensions={0} | all-to-all | bytes 589824 | tf_op jit(solution)/shard_map/all_to_all | solution.py:52
  34.3 0.7 all-gather.6.cloned.1.call-update
  35.2 2.2 scatter_custom_fusion
  37.5 9.9 %all_to_all.38 = bf16[8,1,48]{2,1,0:T(2,128)(2,1)S(1)} all-to-all(bf16[8,1,48]{2,1,0:T(2,128)(2,1)S(1)} %all_to_all.32), channel_id=1, replica_groups=mesh['dp'=8,'expert'=8,'etp'=8] {'expert'}, dimensions={0} | all-to-all | bytes 1536 | tf_op jit(solution)/shard_map/all_to_all | solution.py:59
  47.5 48.7 %all-gather.4.cloned.1.call-done = bf16[384,3072]{1,0:T(8,128)(2,1)} async-done(((bf16[384,384]{1,0:T(8,128)(2,1)}), bf16[384,3072]{1,0:T(8,128)(2,1)}) %all-gather.4.cloned.1.call-update) | async-done | bytes 2359312 | tf_op jit(solution)/shard_map/all_gather | solution.py:61
  96.2 79.4 %all-gather.6.cloned.1.call-done = bf16[1,1024,3072]{2,1,0:T(8,128)(2,1)} async-done(((bf16[1,1024,384]{2,1,0:T(8,128)(2,1)}), bf16[1,1024,3072]{2,1,0:T(8,128)(2,1)}) %all-gather.6.cloned.1.call-update) | async-done | bytes 6291472 | tf_op jit(solution)/shard_map/all_gather | solution.py:66
  175.6 8.6 %multiply_reduce_fusion = (f32[384]{0:T(512)S(1)}, bf16[384,1024]{1,0:T(8,128)(2,1)}, bf16[384,1024]{1,0:T(8,128)(2,1)}, f32[384,1024]{1,0:T(8,128)}) fusion(bf16[1,1,8,48,1024]{4,3,2,1,0:T(8,128)(2,1)} %param.10, bf16[1,1,8,48,1024]{4,3,2,1,0:T(8,128)(2,1)S(1)} %copy-done.2, f32[384]{0:T(512)S(1)} %reshape.116, ...), kind=kOutput, calls=%fused_computation.21 | convolution fusion | flops 2423389696 | bytes 13372416 | tf_op jit(solution)/shard_map/dot_general | solution.py:64
  184.3 16.5 %psum.7 = f32[8,1,48]{2,1,0:T(1,128)} all-reduce(f32[8,1,48]{2,1,0:T(1,128)S(1)} %all_to_all.28), channel_id=1, replica_groups=mesh['dp'=8,'expert'=8,'etp'=8] {'etp'}, use_global_device_ids=true, to_apply=%region_6.7 | all-reduce | flops 384 | bytes 3072 | tf_op jit(solution)/shard_map/psum | solution.py:76
  200.7 10.3 %all-to-all-start.2 = ((f32[8,1,48]{2,1,0:T(1,128)}), f32[8,1,48]{2,1,0:T(1,128)S(1)}, u32[]{:S(2)}, u32[]{:S(2)}) async-start(f32[8,1,48]{2,1,0:T(1,128)} %psum.7), calls=%async_computation.2 | async-start | bytes 8192 | tf_op jit(solution)/shard_map/all_to_all | solution.py:77
  211.0 5.5 %convolution_convert_fusion = bf16[1024,3072]{1,0:T(8,128)(2,1)S(1)} fusion(bf16[384,3072]{1,0:T(8,128)(2,1)S(1)} %copy-done.1, f32[384]{0:T(512)S(1)} %reshape.116, f32[384,1024]{1,0:T(8,128)} %get-tuple-element.15, bf16[384,1024]{1,0:T(8,128)(2,1)} %bitcast.48), kind=kOutput, calls=%fused_computation.6 | convolution fusion | flops 2423783424 | bytes 11011584 | tf_op jit(solution)/shard_map/dot_general | solution.py:85
  216.6 3.3 copy.24
  219.9 4.7 %all-to-all-start.3 = ((bf16[1024,8,384]{2,0,1:T(8,128)(2,1)}), bf16[1024,8,384]{2,0,1:T(8,128)(2,1)}, u32[]{:S(2)}, u32[]{:S(2)}) async-start(bf16[1024,8,384]{2,0,1:T(8,128)(2,1)} %bitcast.39), calls=%async_computation.3 | async-start | bytes 12582912 | tf_op jit(solution)/shard_map/all_to_all | solution.py:88
  224.7 0.5 broadcast.72
  225.2 0.7 reduce.12
  225.9 1.9 gather_fusion
  228.0 0.6 copy.21
  228.7 137.9 %all-to-all-done.3 = bf16[1024,8,384]{2,0,1:T(8,128)(2,1)} async-done(((bf16[1024,8,384]{2,0,1:T(8,128)(2,1)}), bf16[1024,8,384]{2,0,1:T(8,128)(2,1)}, u32[]{:S(2)}, u32[]{:S(2)}) %all-to-all-start.3) | async-done | bytes 6291488 | tf_op jit(solution)/shard_map/all_to_all | solution.py:88
  366.6 4.7 %reduce_sum.35 = bf16[1024,384]{1,0:T(8,128)(2,1)} reduce(bf16[1024,8,384]{2,0,1:T(8,128)(2,1)} %all-to-all-done.3, bf16[]{:T(256)} %constant.6.clone.1), dimensions={1}, to_apply=%region_7.8 | reduce | flops 2752512 | bytes 7077890 | tf_op jit(solution)/shard_map/reduce_sum | solution.py:89
  (29 shorter events, 1.6 us)
Async XLA Ops:
  7.2 27.8 %copy-start = (bf16[128,2]{0,1:T(2,128)(2,1)S(1)}, bf16[128,2]{0,1:T(2,128)(2,1)}, u32[]{:S(2)}) copy-start(bf16[128,2]{0,1:T(2,128)(2,1)} %param.8) | copy-start | bytes 1540
  7.2 89.0 %all-gather.4.cloned.1.call-start = ((), (), s32[]{:S(2)}) async-start(), calls=%async_computation.4 | async-start | bytes 2654208 | tf_op jit(solution)/shard_map/all_gather | solution.py:61
  7.9 167.7 %copy-start.2 = (bf16[1,1,8,48,1024]{4,3,2,1,0:T(8,128)(2,1)S(1)}, bf16[1,1,8,48,1024]{4,3,2,1,0:T(8,128)(2,1)}, u32[]{:S(2)}) copy-start(bf16[1,1,8,48,1024]{4,3,2,1,0:T(8,128)(2,1)} %param.9) | copy-start | bytes 2359300
  34.2 141.4 %all-gather.6.cloned.1.call-start = ((), (), s32[]{:S(2)}) async-start(), calls=%async_computation.5 | async-start | bytes 7077888 | tf_op jit(solution)/shard_map/all_gather | solution.py:66
  96.2 114.8 %copy-start.1 = (bf16[384,3072]{1,0:T(8,128)(2,1)S(1)}, bf16[384,3072]{1,0:T(8,128)(2,1)}, u32[]{:S(2)}) copy-start(bf16[384,3072]{1,0:T(8,128)(2,1)} %all-gather.4.cloned.1.call-done) | copy-start | bytes 7077892
  200.7 19.2 %all-to-all-start.2 = ((f32[8,1,48]{2,1,0:T(1,128)}), f32[8,1,48]{2,1,0:T(1,128)S(1)}, u32[]{:S(2)}, u32[]{:S(2)}) async-start(f32[8,1,48]{2,1,0:T(1,128)} %psum.7), calls=%async_computation.2 | async-start | bytes 8192 | tf_op jit(solution)/shard_map/all_to_all | solution.py:77
  219.9 146.6 %all-to-all-start.3 = ((bf16[1024,8,384]{2,0,1:T(8,128)(2,1)}), bf16[1024,8,384]{2,0,1:T(8,128)(2,1)}, u32[]{:S(2)}, u32[]{:S(2)}) async-start(bf16[1024,8,384]{2,0,1:T(8,128)(2,1)} %bitcast.39), calls=%async_computation.3 | async-start | bytes 12582912 | tf_op jit(solution)/shard_map/all_to_all | solution.py:88
Sparse Core Ops, SparseCore 0:
  34.3 61.8 all-gather.3
  98.3 77.2 all-gather.5
where the time goes:
time: 379 us; the launch traced here: 378 us
  waiting for transfers between devices  267 us (70%)
  blocking collectives  47.6 us (13%)
  starting transfers between devices  15.1 us (4%)
  matrix products  14.2 us (4%)
  between operations  14.2 us (4%)
  local copies, waits for them, and re-layouts  13.6 us (4%)
  other arithmetic  6.84 us (2%)
    all_to_all x1, waiting for transfers between devices, per_device(): lax.all_to_all(partial_value, 'dp', split_axis=1, concat_axis=0, tiled=True)  138 us
    all_gather x1, waiting for transfers between devices, per_device(): lax.all_gather(weight, 'dp', axis=1, tiled=True)  79.4 us
    all_gather x1, waiting for transfers between devices, per_device(): lax.all_gather(routed.reshape(slot_count, -1), 'etp', axis=1, tiled=True)  48.7 us
    all_to_all x1, blocking collectives, per_device(): lax.all_to_all(send_rows.reshape(experts, capacity, -1), 'expert', split_...  21.3 us
    psum x1, blocking collectives, per_device(): row_terms = lax.psum(row_terms, 'etp')  16.5 us
    all_to_all x1, starting transfers between devices, per_device(): lax.all_to_all(row_terms.reshape(experts, capacity), 'expert', split_axis...  10.3 us
    all_to_all x1, blocking collectives, per_device(): lax.all_to_all(send_mix, 'expert', split_axis=0, concat_axis=0, tiled=True)  9.91 us
    dot_general x1, matrix products, per_device(): lax.dot_general(routed, lax.all_gather(weight, 'dp', axis=1, tiled=True),...  8.61 us
  transfers between devices with their start and end apart: 4, of which 3 were waited for; matrix products, arithmetic and copies ran while one was open for 4% of the time, Pallas kernels for 0%

commit v1 on v0

v1 whole, which is shorter than its diff:
```python
import jax
import jax.numpy as jnp
from jax import lax
from jax.experimental import pallas as pl
from jax.experimental.pallas import tpu as pltpu
from jax.sharding import PartitionSpec as P

N = 8
CAP = 48
R = 384
HID = 1024
C = 384
CH = 256
NCH = 4
TOK = 128
MESH = pl.DeviceIdType.MESH


def copy_to(src, dst, send_sem, recv_sem, axis, index):
    return pltpu.make_async_remote_copy(
        src_ref=src,
        dst_ref=dst,
        send_sem=send_sem,
        recv_sem=recv_sem,
        device_id={axis: index},
        device_id_type=MESH,
    )


def kernel(
    x_ref, rm_ref, gate_hbm, up_hbm, w_hbm,
    gg_hbm, gu_hbm, gm_ref, down_hbm,
    wbuf, abuf, xs, ms, mix, onehot, weighted, a2buf, hbuf, hid, upstream, acc,
    gate, up, gg, gu, down, rts, rtr, gms, gmr,
    io_sem, w_send, w_recv, a1_send, a1_recv, m_send, m_recv, a2_send, a2_recv,
    a3_send, a3_recv, a4_send, a4_recv, h_send, h_recv,
    r1_send, r1_recv, r2_send, r2_recv,
):
    z = lax.axis_index("dp")
    me = lax.axis_index("expert")
    h = lax.axis_index("etp")

    def peer(index, offset):
        return lax.rem(index + offset + N, N)

    barrier = pltpu.get_barrier_semaphore()
    for o in range(1, N):
        for axis, index in (("dp", z), ("expert", me), ("etp", h)):
            pl.semaphore_signal(
                barrier, inc=1, device_id={axis: peer(index, o)}, device_id_type=MESH
            )
    pl.semaphore_wait(barrier, 3 * (N - 1))

    loads = [
        pltpu.make_async_copy(w_hbm, wbuf.at[z], io_sem.at[0]),
        pltpu.make_async_copy(gate_hbm, gate, io_sem.at[1]),
        pltpu.make_async_copy(up_hbm, up, io_sem.at[2]),
    ]
    for load in loads:
        load.start()
    loads[0].wait()

    def ring(buf, send, recv, step, chunk):
        way = 1 if chunk < NCH // 2 else -1
        block = peer(z, -way * step)
        part = buf.at[block, pl.ds(chunk * CH, CH)]
        return copy_to(part, part, send.at[chunk, step], recv.at[chunk, step], "dp", peer(z, way))

    def ring_arrival(buf, send, recv, step, chunk):
        way = 1 if chunk < NCH // 2 else -1
        block = peer(z, -way * (step + 1))
        part = buf.at[block, pl.ds(chunk * CH, CH)]
        return copy_to(part, part, send.at[chunk, step], recv.at[chunk, step], "dp", peer(z, way))

    def forward_w(step):
        for chunk in (0, 2, 1, 3):
            if step > 0:
                ring_arrival(wbuf, w_send, w_recv, step - 1, chunk).wait_recv()
            ring(wbuf, w_send, w_recv, step, chunk).start()

    forward_w(0)

    r0, r1 = rm_ref[0:1, :], rm_ref[1:2, :]
    m0, m1 = rm_ref[2:3, :], rm_ref[3:4, :]
    experts = lax.broadcasted_iota(jnp.int32, (N, TOK), 0).astype(jnp.float32)
    named = jnp.where((r0 == experts) | (r1 == experts), 1.0, 0.0)
    before = jnp.where(
        lax.broadcasted_iota(jnp.int32, (TOK, TOK), 0)
        < lax.broadcasted_iota(jnp.int32, (TOK, TOK), 1),
        1.0,
        0.0,
    ).astype(jnp.bfloat16)
    position = jnp.dot(named.astype(jnp.bfloat16), before, preferred_element_type=jnp.float32)
    place = lax.broadcasted_iota(jnp.int32, (CAP, TOK), 0).astype(jnp.float32)
    for e in range(N):
        chosen = jnp.where(
            (place == position[e : e + 1, :]) & (named[e : e + 1, :] > 0.0), 1.0, 0.0
        )
        onehot[e] = chosen
        weights = jnp.where(r0 == float(e), m0, 0.0) + jnp.where(r1 == float(e), m1, 0.0)
        column = jnp.sum(chosen * weights, axis=1, keepdims=True)
        ms[e] = jnp.broadcast_to(column, (CAP, TOK)).astype(jnp.bfloat16)
        xs[e] = jnp.dot(
            chosen.astype(jnp.bfloat16), x_ref[...], preferred_element_type=jnp.float32
        ).astype(jnp.bfloat16)

    def rows_of(index):
        return pl.ds(pl.multiple_of(index * CAP, CAP), CAP)

    def a1(o, arrival=False):
        dst = peer(me, o)
        where = rows_of(peer(me, -o) if arrival else me)
        return (
            copy_to(xs.at[dst], abuf.at[h, where], a1_send.at[o], a1_recv.at[o], "expert", dst),
            copy_to(ms.at[dst], mix.at[where], m_send.at[o], m_recv.at[o], "expert", dst),
        )

    for o in range(1, N):
        for one in a1(o):
            one.start()
    abuf[h, rows_of(me), :] = xs[me]
    mix[rows_of(me), :] = ms[me]

    forward_w(1)
    for o in range(1, N):
        for one in a1(o, arrival=True):
            one.wait_recv()

    def a2(o, arrival=False):
        slot = peer(h, -o) if arrival else h
        return copy_to(
            abuf.at[slot], abuf.at[slot], a2_send.at[o], a2_recv.at[o], "etp", peer(h, o)
        )

    for o in range(1, N):
        a2(o).start()
    forward_w(2)
    forward_w(3)
    forward_w(4)
    for o in range(1, N):
        a2(o, arrival=True).wait_recv()

    share = mix[rows_of(h), 0:1].astype(jnp.float32)
    for k in range(N):
        weighted[k] = (share * abuf[k, rows_of(h), :].astype(jnp.float32)).astype(jnp.bfloat16)

    def a3(o, arrival=False):
        dst = peer(z, o)
        slot = peer(z, -o) if arrival else z
        return copy_to(
            weighted.at[dst], a2buf.at[slot, rows_of(h)], a3_send.at[o], a3_recv.at[o], "dp", dst
        )

    for o in range(1, N):
        a3(o).start()
    a2buf[z, rows_of(h), :] = weighted[z]
    forward_w(5)
    for o in range(1, N):
        a3(o, arrival=True).wait_recv()

    def a4(o, arrival=False):
        where = rows_of(peer(h, -o) if arrival else h)
        part = a2buf.at[:, where]
        return copy_to(part, part, a4_send.at[o], a4_recv.at[o], "etp", peer(h, o))

    for o in range(1, N):
        a4(o).start()
    forward_w(6)

    def product(block, chunk):
        return lax.dot_general(
            abuf[block],
            wbuf[block, pl.ds(chunk * CH, CH), :],
            (((1,), (1,)), ((), ())),
            preferred_element_type=jnp.float32,
        )

    for chunk in range(NCH):
        way = 1 if chunk < NCH // 2 else -1
        upstream[chunk] = product(z, chunk)

        def add(step, carry, chunk=chunk, way=way):
            upstream[chunk] += product(peer(z, -way * step), chunk)
            return carry

        lax.fori_loop(1, N - 1, add, 0)

    loads[1].wait()
    loads[2].wait()
    RB = 64

    def terms_of(chunk):
        columns = pl.ds(chunk * CH, CH)

        def rows(i, carry):
            where = pl.ds(pl.multiple_of(i * RB, RB), RB)
            a = gate[where, columns].astype(jnp.float32)
            b = up[where, columns].astype(jnp.float32)
            u = upstream[chunk, where, :]
            share = mix[where, 0:1].astype(jnp.float32)
            sig = jax.nn.sigmoid(a)
            silu = a * sig
            hidden = silu * b
            scaled = share * u
            gg[where, columns] = (scaled * b * sig * (1.0 + a * (1.0 - sig))).astype(jnp.bfloat16)
            gu[where, columns] = (scaled * silu).astype(jnp.bfloat16)
            hid[where, :] = hidden.astype(jnp.bfloat16)
            row_sum = jnp.broadcast_to(jnp.sum(u * hidden, axis=1, keepdims=True), (RB, TOK))
            if chunk == 0:
                rts[where, :] = row_sum
            else:
                rts[where, :] += row_sum
            return carry

        lax.fori_loop(0, R // RB, rows, 0)

    for chunk in (0, 2, 1, 3):
        way = 1 if chunk < NCH // 2 else -1
        ring_arrival(wbuf, w_send, w_recv, N - 2, chunk).wait_recv()
        upstream[chunk] += product(peer(z, -way * (N - 1)), chunk)
        terms_of(chunk)
        hbuf[z, pl.ds(chunk * CH, CH), :] = hid[...].T
        ring(hbuf, h_send, h_recv, 0, chunk).start()

    stores = [
        pltpu.make_async_copy(gg, gg_hbm, io_sem.at[3]),
        pltpu.make_async_copy(gu, gu_hbm, io_sem.at[4]),
    ]
    for store in stores:
        store.start()

    def r1_copy(o, arrival=False):
        dst = peer(me, o)
        slot = peer(me, -o) if arrival else me
        return copy_to(
            rts.at[rows_of(dst)], rtr.at[slot], r1_send.at[o], r1_recv.at[o], "expert", dst
        )

    for o in range(1, N):
        r1_copy(o).start()
    rtr[me] = rts[rows_of(me), :]
    for o in range(1, N):
        a4(o, arrival=True).wait_recv()

    def grad(block, chunk):
        return jnp.dot(
            hbuf[block, pl.ds(chunk * CH, CH), :],
            a2buf[block],
            preferred_element_type=jnp.float32,
        )

    for chunk in range(NCH):
        acc[chunk] = grad(z, chunk)
    for o in range(1, N):
        r1_copy(o, arrival=True).wait_recv()
    gm0 = jnp.zeros((1, TOK), jnp.float32)
    gm1 = jnp.zeros((1, TOK), jnp.float32)
    for e in range(N):
        picked = jnp.sum(onehot[e] * rtr[e], axis=0, keepdims=True)
        gm0 += jnp.where(r0 == float(e), picked, 0.0)
        gm1 += jnp.where(r1 == float(e), picked, 0.0)
    row = lax.broadcasted_iota(jnp.int32, (N, TOK), 0)
    gms[...] = jnp.where(row == 0, gm0, jnp.where(row == 1, gm1, 0.0))

    def r2_copy(o, arrival=False):
        slot = peer(h, -o) if arrival else h
        return copy_to(gms, gmr.at[slot], r2_send.at[o], r2_recv.at[o], "etp", peer(h, o))

    for o in range(1, N):
        r2_copy(o).start()
    gmr[h] = gms[...]

    for step in range(1, N):
        for chunk in (0, 2, 1, 3):
            way = 1 if chunk < NCH // 2 else -1
            ring_arrival(hbuf, h_send, h_recv, step - 1, chunk).wait_recv()
            if step < N - 1:
                ring(hbuf, h_send, h_recv, step, chunk).start()
            else:
                down[pl.ds(chunk * CH, CH), :] = (
                    acc[chunk] + grad(peer(z, -way * step), chunk)
                ).astype(jnp.bfloat16)
                pltpu.make_async_copy(
                    down.at[pl.ds(chunk * CH, CH)],
                    down_hbm.at[pl.ds(chunk * CH, CH)],
                    io_sem.at[5 + chunk],
                ).start()
        if step < N - 1:
            for chunk in range(NCH):
                way = 1 if chunk < NCH // 2 else -1
                acc[chunk] += grad(peer(z, -way * step), chunk)
        if step == 1:
            for o in range(1, N):
                r2_copy(o, arrival=True).wait_recv()
            gm_ref[...] = jnp.sum(gmr[...], axis=0)

    for store in stores:
        store.wait()
    for chunk in range(NCH):
        pltpu.make_async_copy(
            down.at[pl.ds(chunk * CH, CH)],
            down_hbm.at[pl.ds(chunk * CH, CH)],
            io_sem.at[5 + chunk],
        ).wait()
    for step in range(N - 1):
        for chunk in range(NCH):
            ring(wbuf, w_send, w_recv, step, chunk).wait_send()
            ring(hbuf, h_send, h_recv, step, chunk).wait_send()
    for o in range(1, N):
        for one in a1(o):
            one.wait_send()
        a2(o).wait_send()
        a3(o).wait_send()
        a4(o).wait_send()
        r1_copy(o).wait_send()
        r2_copy(o).wait_send()


def per_device(grad_out, routing, mix_weights, gate_pre, up_pre, down_weight):
    rm = jnp.concatenate(
        [routing.astype(jnp.float32).T, mix_weights.astype(jnp.float32).T], axis=0
    )
    rm = jnp.pad(rm, ((0, 4), (0, 0)))
    vmem = pl.BlockSpec(memory_space=pltpu.VMEM)
    hbm = pl.BlockSpec(memory_space=pl.ANY)
    bf16, f32 = jnp.bfloat16, jnp.float32
    dma = pltpu.SemaphoreType.DMA
    gg, gu, gm, down = pl.pallas_call(
        kernel,
        out_shape=(
            jax.ShapeDtypeStruct((R, HID), bf16),
            jax.ShapeDtypeStruct((R, HID), bf16),
            jax.ShapeDtypeStruct((N, TOK), f32),
            jax.ShapeDtypeStruct((HID, C), bf16),
        ),
        in_specs=[vmem, vmem, hbm, hbm, hbm],
        out_specs=(hbm, hbm, vmem, hbm),
        scratch_shapes=[
            pltpu.VMEM((N, HID, C), bf16),
            pltpu.VMEM((N, R, C), bf16),
            pltpu.VMEM((N, CAP, C), bf16),
            pltpu.VMEM((N, CAP, TOK), bf16),
            pltpu.VMEM((R, TOK), bf16),
            pltpu.VMEM((N, CAP, TOK), f32),
            pltpu.VMEM((N, CAP, C), bf16),
            pltpu.VMEM((N, R, C), bf16),
            pltpu.VMEM((N, HID, R), bf16),
            pltpu.VMEM((R, CH), bf16),
            pltpu.VMEM((NCH, R, CH), f32),
            pltpu.VMEM((NCH, CH, C), f32),
            pltpu.VMEM((R, HID), bf16),
            pltpu.VMEM((R, HID), bf16),
            pltpu.VMEM((R, HID), bf16),
            pltpu.VMEM((R, HID), bf16),
            pltpu.VMEM((HID, C), bf16),
            pltpu.VMEM((R, TOK), f32),
            pltpu.VMEM((N, CAP, TOK), f32),
            pltpu.VMEM((N, TOK), f32),
            pltpu.VMEM((N, N, TOK), f32),
            dma((9,)),
            dma((NCH, N)), dma((NCH, N)),
            dma((N,)), dma((N,)),
            dma((N,)), dma((N,)),
            dma((N,)), dma((N,)),
            dma((N,)), dma((N,)),
            dma((N,)), dma((N,)),
            dma((NCH, N)), dma((NCH, N)),
            dma((N,)), dma((N,)),
            dma((N,)), dma((N,)),
        ],
        compiler_params=pltpu.CompilerParams(
            collective_id=0, has_side_effects=True, vmem_limit_bytes=56 * 1024 * 1024
        ),
        cost_estimate=pl.CostEstimate(
            flops=4 * R * HID * C * N, bytes_accessed=6 * HID * C * 2, transcendentals=R * HID
        ),
    )(
        grad_out,
        rm,
        gate_pre.reshape(R, HID),
        up_pre.reshape(R, HID),
        down_weight.reshape(HID, C),
    )
    return (
        gg.reshape(gate_pre.shape),
        gu.reshape(gate_pre.shape),
        gm[0:2].T,
        down[None],
    )


def solution(mesh):
    in_specs = (
        P(("dp", "expert"), "etp"),
        P(("dp", "expert"), None),
        P(("dp", "expert"), None),
        P("dp", "expert", None, None, "etp"),
        P("dp", "expert", None, None, "etp"),
        P("expert", "etp", "dp"),
    )
    out_specs = (
        P("dp", "expert", None, None, "etp"),
        P("dp", "expert", None, None, "etp"),
        P(("dp", "expert"), None),
        P("expert", "etp", "dp"),
    )
    return jax.shard_map(
        per_device, mesh=mesh, in_specs=in_specs, out_specs=out_specs, check_vma=False
    )
```

time: 379 us -> 165 us (0.44)
  waiting for transfers between devices: 267 us -> 0 us
  Pallas kernels: 0 us -> 156 us
  blocking collectives: 47.6 us -> 0 us
  starting transfers between devices: 15.1 us -> 0 us
  matrix products: 14.2 us -> 0 us
  between operations: 14.2 us -> 0.65 us
  local copies, waits for them, and re-layouts: 13.6 us -> 7 us
  other arithmetic: 6.84 us -> 0.61 us
    pallas_call x0 -> x1, Pallas kernels: none -> 156 us  [per_device(): pl.pallas_call(kernel, out_shape=(jax.ShapeDtypeStruct((R, HID), bf16), j...]
    all_to_all x2 -> x0, waiting for transfers between devices: 138 us -> none  [the longest x1 138 us: per_device(): lax.all_to_all(partial_value, 'dp', split_axis=1, concat_axis=0, tiled=True)]
    all_gather x2 -> x0, waiting for transfers between devices: 128 us -> none  [the longest x1 79.4 us: per_device(): lax.all_gather(weight, 'dp', axis=1, tiled=True)]
    all_to_all x2 -> x0, blocking collectives: 31.2 us -> none  [the longest x1 21.3 us: per_device(): lax.all_to_all(send_rows.reshape(experts, capacity, -1), 'expert', split_...]
    psum x1 -> x0, blocking collectives: 16.5 us -> none  [per_device(): row_terms = lax.psum(row_terms, 'etp')]
    all_to_all x2 -> x0, starting transfers between devices: 15 us -> none  [the longest x1 10.3 us: per_device(): lax.all_to_all(row_terms.reshape(experts, capacity), 'expert', split_axis...]
    dot_general x2 -> x0, matrix products: 14.2 us -> none  [the longest x1 8.61 us: per_device(): lax.dot_general(routed, lax.all_gather(weight, 'dp', axis=1, tiled=True),...]
    reduce_sum x2 -> x0, other arithmetic: 4.83 us -> none  [the longest x1 4.74 us: per_device(): jnp.sum(blocks.reshape(replicas, hidden_here, width_here).astype(jnp.floa...]
  transfers between devices with their start and end apart: 4 -> 0, of which waited for: 3 -> 0; matrix products, arithmetic and copies ran while one was open for 4% -> 0% of each run, Pallas kernels for 0% -> 0%
where the time goes in v1:
time: 165 us; the launch traced here: 164 us
  Pallas kernels  156 us (95%)
  local copies, waits for them, and re-layouts  7 us (4%)
    pallas_call x1, Pallas kernels, per_device(): pl.pallas_call(kernel, out_shape=(jax.ShapeDtypeStruct((R, HID), bf16), j...  156 us
    unnamed x11, local copies, waits for them, and re-layouts  5.76 us

profile of v1, /device:TPU:1, one launch (start us, length us, event | category | flops | bytes accessed | tf_op | source)
XLA Modules:
  0.0 164.4 jit_solution(14373175072778800606)
XLA Ops:
  0.6 0.0 copy-start.2
  0.6 0.7 copy-done.2
  1.3 0.0 copy-start.3
  1.3 0.7 copy-done.3
  2.0 0.6 select_maximum_fusion.rm_ref
  2.6 156.2 %shard_map.93 = (bf16[384,1024]{1,0:T(8,128)(2,1)}, bf16[384,1024]{1,0:T(8,128)(2,1)}, f32[8,128]{1,0:T(8,128)}, bf16[1024,384]{1,0:T(8,128)(2,1)}) custom-call(bf16[128,384]{1,0:T(8,128)(2,1)} %x_ref.1, f32[8,128]{1,0:T(8,128)} %select_maximum_fusion.rm_ref, bf16[384,1024]{1,0:T(8,128)(2,1)} %bitcast.15, bf16[384,1024]{1,0:T(8,128)(2,1)} %bitcast.16, ...), custom_call_target="tpu_custom_call" | custom-call | flops 4831838208 | bytes 4718592 | tf_op jit(solution)/shard_map/pallas_call | solution.py:328
  158.8 1.2 slice_bitcast_fusion
  160.0 0.0 copy-start.1
  160.0 2.1 %copy.13 = bf16[1,1,8,48,1024]{4,3,2,1,0:T(8,128)(2,1)} copy(bf16[1,1,8,48,1024]{4,3,2,1,0:T(8,128)(2,1)} %bitcast.14) | data formatting | bytes 1572864
  162.1 0.0 copy-done.1
  162.1 0.0 copy-start
  162.1 0.9 copy.14
  163.0 0.5 copy-done
  163.6 0.9 copy.15
  (2 shorter events, 0.0 us)
Async XLA Ops:
  0.6 0.7 copy-start.2
  1.3 0.7 copy-start.3
  160.0 2.1 %copy-start.1 = (bf16[384,1024]{1,0:T(8,128)(2,1)S(1)}, bf16[384,1024]{1,0:T(8,128)(2,1)}, u32[]{:S(2)}) copy-start(bf16[384,1024]{1,0:T(8,128)(2,1)} %get-tuple-element.9) | copy-start | bytes 2359300
  162.1 1.4 copy-start

commit v2 on v1

--- a/solution.py
+++ b/solution.py
@@ -12,6 +12,11 @@
 C = 384
 CH = 256
 NCH = 4
+SUB = 128
+NSUB = 8
+SEG = 4
+PLANE = (0, 1, 2, 3, 3, 3, 0, 0)
+ROLE = (0, 0, 0, 0, 1, 2, 2, 1)
 TOK = 128
 MESH = pl.DeviceIdType.MESH
 
@@ -31,10 +36,10 @@
     x_ref, rm_ref, gate_hbm, up_hbm, w_hbm,
     gg_hbm, gu_hbm, gm_ref, down_hbm,
     wbuf, abuf, xs, ms, mix, onehot, weighted, a2buf, hbuf, hid, upstream, acc,
-    gate, up, gg, gu, down, rts, rtr, gms, gmr,
+    gate, up, gg, gu, down, psend, precv, rts, rtr, gms, gmr,
     io_sem, w_send, w_recv, a1_send, a1_recv, m_send, m_recv, a2_send, a2_recv,
     a3_send, a3_recv, a4_send, a4_recv, h_send, h_recv,
-    r1_send, r1_recv, r2_send, r2_recv,
+    p_send, p_recv, r1_send, r1_recv, r2_send, r2_recv,
 ):
     z = lax.axis_index("dp")
     me = lax.axis_index("expert")
@@ -42,6 +47,11 @@
 
     def peer(index, offset):
         return lax.rem(index + offset + N, N)
+
+    pos = lax.rem(z + 2 * lax.rem(me, 2), SEG)
+    start = peer(z, -pos)
+    outer = (pos == 0) | (pos == SEG - 1)
+    outward = jnp.where(pos == 0, -1, 1)
 
     barrier = pltpu.get_barrier_semaphore()
     for o in range(1, N):
@@ -141,30 +151,60 @@
         a2(o, arrival=True).wait_recv()
 
     share = mix[rows_of(h), 0:1].astype(jnp.float32)
-    for k in range(N):
-        weighted[k] = (share * abuf[k, rows_of(h), :].astype(jnp.float32)).astype(jnp.bfloat16)
-
-    def a3(o, arrival=False):
-        dst = peer(z, o)
-        slot = peer(z, -o) if arrival else z
+    for o in range(N):
+        weighted[o] = (
+            share * abuf[peer(start, o), rows_of(h), :].astype(jnp.float32)
+        ).astype(jnp.bfloat16)
+
+    def a3(o):
         return copy_to(
-            weighted.at[dst], a2buf.at[slot, rows_of(h)], a3_send.at[o], a3_recv.at[o], "dp", dst
-        )
-
-    for o in range(1, N):
-        a3(o).start()
-    a2buf[z, rows_of(h), :] = weighted[z]
+            weighted.at[o],
+            a2buf.at[ROLE[o], pos, rows_of(h)],
+            a3_send.at[o],
+            a3_recv.at[ROLE[o], pos],
+            "dp",
+            peer(start, PLANE[o]),
+        )
+
+    for o in range(N):
+
+        @pl.when(pos != PLANE[o])
+        def _(o=o):
+            a3(o).start()
+
+        @pl.when(pos == PLANE[o])
+        def _(o=o):
+            a2buf[ROLE[o], pos, rows_of(h), :] = weighted[o]
+
     forward_w(5)
-    for o in range(1, N):
-        a3(o, arrival=True).wait_recv()
-
-    def a4(o, arrival=False):
+    for role in range(3):
+        for source in range(SEG):
+
+            @pl.when((pos != source) & ((role == 0) | outer))
+            def _(role=role, source=source):
+                part = a2buf.at[role, source, rows_of(h)]
+                copy_to(
+                    part, part, a3_send.at[0], a3_recv.at[role, source], "dp", peer(start, source)
+                ).wait_recv()
+
+    def a4(o, role, arrival=False):
         where = rows_of(peer(h, -o) if arrival else h)
-        part = a2buf.at[:, where]
-        return copy_to(part, part, a4_send.at[o], a4_recv.at[o], "etp", peer(h, o))
-
-    for o in range(1, N):
-        a4(o).start()
+        part = a2buf.at[role, :, where]
+        return copy_to(
+            part, part, a4_send.at[role, o], a4_recv.at[role, o], "etp", peer(h, o)
+        )
+
+    def each_a4(act):
+        for o in range(1, N):
+            act(o, 0)
+
+        @pl.when(outer)
+        def _():
+            for o in range(1, N):
+                act(o, 1)
+                act(o, 2)
+
+    each_a4(lambda o, role: a4(o, role).start())
     forward_w(6)
 
     def product(block, chunk):
@@ -214,104 +254,176 @@
 
         lax.fori_loop(0, R // RB, rows, 0)
 
-    for chunk in (0, 2, 1, 3):
-        way = 1 if chunk < NCH // 2 else -1
-        ring_arrival(wbuf, w_send, w_recv, N - 2, chunk).wait_recv()
-        upstream[chunk] += product(peer(z, -way * (N - 1)), chunk)
-        terms_of(chunk)
-        hbuf[z, pl.ds(chunk * CH, CH), :] = hid[...].T
-        ring(hbuf, h_send, h_recv, 0, chunk).start()
-
-    stores = [
-        pltpu.make_async_copy(gg, gg_hbm, io_sem.at[3]),
-        pltpu.make_async_copy(gu, gu_hbm, io_sem.at[4]),
-    ]
-    for store in stores:
-        store.start()
-
-    def r1_copy(o, arrival=False):
-        dst = peer(me, o)
-        slot = peer(me, -o) if arrival else me
+    def h_copy(step, sub, way, arrival=False):
+        block = pos - way * (step + 1 if arrival else step)
+        part = hbuf.at[block, pl.ds(sub * SUB, SUB)]
+        side = 0 if way > 0 else 1
         return copy_to(
-            rts.at[rows_of(dst)], rtr.at[slot], r1_send.at[o], r1_recv.at[o], "expert", dst
-        )
-
-    for o in range(1, N):
-        r1_copy(o).start()
-    rtr[me] = rts[rows_of(me), :]
-    for o in range(1, N):
-        a4(o, arrival=True).wait_recv()
-
-    def grad(block, chunk):
-        return jnp.dot(
-            hbuf[block, pl.ds(chunk * CH, CH), :],
-            a2buf[block],
-            preferred_element_type=jnp.float32,
-        )
-
-    for chunk in range(NCH):
-        acc[chunk] = grad(z, chunk)
-    for o in range(1, N):
-        r1_copy(o, arrival=True).wait_recv()
-    gm0 = jnp.zeros((1, TOK), jnp.float32)
-    gm1 = jnp.zeros((1, TOK), jnp.float32)
-    for e in range(N):
-        picked = jnp.sum(onehot[e] * rtr[e], axis=0, keepdims=True)
-        gm0 += jnp.where(r0 == float(e), picked, 0.0)
-        gm1 += jnp.where(r1 == float(e), picked, 0.0)
-    row = lax.broadcasted_iota(jnp.int32, (N, TOK), 0)
-    gms[...] = jnp.where(row == 0, gm0, jnp.where(row == 1, gm1, 0.0))
-
-    def r2_copy(o, arrival=False):
-        slot = peer(h, -o) if arrival else h
-        return copy_to(gms, gmr.at[slot], r2_send.at[o], r2_recv.at[o], "etp", peer(h, o))
-
-    for o in range(1, N):
-        r2_copy(o).start()
-    gmr[h] = gms[...]
-
-    for step in range(1, N):
-        for chunk in (0, 2, 1, 3):
+            part, part, h_send.at[side, step, sub], h_recv.at[side, step, sub], "dp", peer(z, way)
+        )
+
+    def sends(step, way):
+        if way > 0:
+            return (pos >= step) & (pos < SEG - 1)
+        return (pos < SEG - step) & (pos > 0)
+
+    def receives(step, way):
+        return (pos > step) if way > 0 else (pos < SEG - 1 - step)
+
+    def h_step(step, sub):
+        for way in (1, -1):
+            if step > 0:
+
+                @pl.when(receives(step - 1, way))
+                def _(way=way):
+                    h_copy(step - 1, sub, way, arrival=True).wait_recv()
+
+            if step < SEG - 1:
+
+                @pl.when(sends(step, way))
+                def _(way=way):
+                    h_copy(step, sub, way).start()
+
+    def grad(role, sub):
+        total = None
+        for block in range(SEG):
+            term = jnp.dot(
+                hbuf[block, pl.ds(sub * SUB, SUB), :],
+                a2buf[role, block],
+                preferred_element_type=jnp.float32,
+            )
+            total = term if total is None else total + term
+        return total
+
+    def partial(role, sub):
+        return copy_to(
+            psend.at[role - 1, pl.ds(sub * SUB, SUB)],
+            precv.at[pl.ds(sub * SUB, SUB)],
+            p_send.at[role - 1, sub],
+            p_recv.at[sub],
+            "dp",
+            peer(z, role * outward),
+        )
+
+    def finish(sub):
+        h_step(SEG - 1, sub)
+
+        @pl.when(outer)
+        def _():
+            for role in (2, 1):
+                psend[role - 1, pl.ds(sub * SUB, SUB), :] = grad(role, sub).astype(jnp.bfloat16)
+                partial(role, sub).start()
+
+        acc[sub] = grad(0, sub)
+
+    def store_down(sub):
+        where = pl.ds(sub * SUB, SUB)
+        return pltpu.make_async_copy(down.at[where], down_hbm.at[where], io_sem.at[5 + sub])
+
+    def conclude(sub):
+        partial(1, sub).wait_recv()
+        where = pl.ds(sub * SUB, SUB)
+        down[where, :] = (acc[sub] + precv[where, :].astype(jnp.float32)).astype(jnp.bfloat16)
+        store_down(sub).start()
+
+    order = (0, 2, 1, 3)
+
+    def subs(turn):
+        return (2 * order[turn], 2 * order[turn] + 1)
+
+    for turn in range(NCH + SEG):
+        if turn < NCH:
+            chunk = order[turn]
             way = 1 if chunk < NCH // 2 else -1
-            ring_arrival(hbuf, h_send, h_recv, step - 1, chunk).wait_recv()
-            if step < N - 1:
-                ring(hbuf, h_send, h_recv, step, chunk).start()
-            else:
-                down[pl.ds(chunk * CH, CH), :] = (
-                    acc[chunk] + grad(peer(z, -way * step), chunk)
-                ).astype(jnp.bfloat16)
-                pltpu.make_async_copy(
-                    down.at[pl.ds(chunk * CH, CH)],
-                    down_hbm.at[pl.ds(chunk * CH, CH)],
-                    io_sem.at[5 + chunk],
-                ).start()
-        if step < N - 1:
-            for chunk in range(NCH):
-                way = 1 if chunk < NCH // 2 else -1
-                acc[chunk] += grad(peer(z, -way * step), chunk)
-        if step == 1:
+            ring_arrival(wbuf, w_send, w_recv, N - 2, chunk).wait_recv()
+            upstream[chunk] += product(peer(z, -way * (N - 1)), chunk)
+            terms_of(chunk)
+            hbuf[pos, pl.ds(chunk * CH, CH), :] = hid[...].T
+            for sub in subs(turn):
+                h_step(0, sub)
+        for step in (1, 2):
+            if 0 <= turn - step < NCH:
+                for sub in subs(turn - step):
+                    h_step(step, sub)
+        if turn == SEG - 1:
+            stores = [
+                pltpu.make_async_copy(gg, gg_hbm, io_sem.at[3]),
+                pltpu.make_async_copy(gu, gu_hbm, io_sem.at[4]),
+            ]
+            for store in stores:
+                store.start()
+
+            def r1_copy(o, arrival=False):
+                dst = peer(me, o)
+                slot = peer(me, -o) if arrival else me
+                return copy_to(
+                    rts.at[rows_of(dst)], rtr.at[slot], r1_send.at[o], r1_recv.at[o], "expert", dst
+                )
+
             for o in range(1, N):
-                r2_copy(o, arrival=True).wait_recv()
-            gm_ref[...] = jnp.sum(gmr[...], axis=0)
+                r1_copy(o).start()
+            rtr[me] = rts[rows_of(me), :]
+            each_a4(lambda o, role: a4(o, role, arrival=True).wait_recv())
+        if 0 <= turn - 3 < NCH:
+            for sub in subs(turn - 3):
+                finish(sub)
+        if turn == SEG + 1:
+            for o in range(1, N):
+                r1_copy(o, arrival=True).wait_recv()
+            gm0 = jnp.zeros((1, TOK), jnp.float32)
+            gm1 = jnp.zeros((1, TOK), jnp.float32)
+            for e in range(N):
+                picked = jnp.sum(onehot[e] * rtr[e], axis=0, keepdims=True)
+                gm0 += jnp.where(r0 == float(e), picked, 0.0)
+                gm1 += jnp.where(r1 == float(e), picked, 0.0)
+            row = lax.broadcasted_iota(jnp.int32, (N, TOK), 0)
+            gms[...] = jnp.where(row == 0, gm0, jnp.where(row == 1, gm1, 0.0))
+
+            def r2_copy(o, arrival=False):
+                slot = peer(h, -o) if arrival else h
+                return copy_to(gms, gmr.at[slot], r2_send.at[o], r2_recv.at[o], "etp", peer(h, o))
+
+            for o in range(1, N):
+                r2_copy(o).start()
+            gmr[h] = gms[...]
+        if 0 <= turn - 4 < NCH:
+            for sub in subs(turn - 4):
+                conclude(sub)
+    for o in range(1, N):
+        r2_copy(o, arrival=True).wait_recv()
+    gm_ref[...] = jnp.sum(gmr[...], axis=0)
 
     for store in stores:
         store.wait()
-    for chunk in range(NCH):
-        pltpu.make_async_copy(
-            down.at[pl.ds(chunk * CH, CH)],
-            down_hbm.at[pl.ds(chunk * CH, CH)],
-            io_sem.at[5 + chunk],
-        ).wait()
+    for sub in range(NSUB):
+        store_down(sub).wait()
+        for way in (1, -1):
+            for step in range(SEG - 1):
+
+                @pl.when(sends(step, way))
+                def _(sub=sub, way=way, step=step):
+                    h_copy(step, sub, way).wait_send()
+
+    @pl.when(outer)
+    def _():
+        for sub in range(NSUB):
+            partial(1, sub).wait_send()
+            partial(2, sub).wait_send()
+
+    for o in range(N):
+
+        @pl.when(pos != PLANE[o])
+        def _(o=o):
+            a3(o).wait_send()
+
+    each_a4(lambda o, role: a4(o, role).wait_send())
     for step in range(N - 1):
         for chunk in range(NCH):
             ring(wbuf, w_send, w_recv, step, chunk).wait_send()
-            ring(hbuf, h_send, h_recv, step, chunk).wait_send()
     for o in range(1, N):
         for one in a1(o):
             one.wait_send()
         a2(o).wait_send()
-        a3(o).wait_send()
-        a4(o).wait_send()
         r1_copy(o).wait_send()
         r2_copy(o).wait_send()
 
@@ -343,28 +455,31 @@
             pltpu.VMEM((R, TOK), bf16),
             pltpu.VMEM((N, CAP, TOK), f32),
             pltpu.VMEM((N, CAP, C), bf16),
-            pltpu.VMEM((N, R, C), bf16),
-            pltpu.VMEM((N, HID, R), bf16),
+            pltpu.VMEM((3, SEG, R, C), bf16),
+            pltpu.VMEM((SEG, HID, R), bf16),
             pltpu.VMEM((R, CH), bf16),
             pltpu.VMEM((NCH, R, CH), f32),
-            pltpu.VMEM((NCH, CH, C), f32),
+            pltpu.VMEM((NSUB, SUB, C), f32),
             pltpu.VMEM((R, HID), bf16),
             pltpu.VMEM((R, HID), bf16),
             pltpu.VMEM((R, HID), bf16),
             pltpu.VMEM((R, HID), bf16),
             pltpu.VMEM((HID, C), bf16),
+            pltpu.VMEM((2, HID, C), bf16),
+            pltpu.VMEM((HID, C), bf16),
             pltpu.VMEM((R, TOK), f32),
             pltpu.VMEM((N, CAP, TOK), f32),
             pltpu.VMEM((N, TOK), f32),
             pltpu.VMEM((N, N, TOK), f32),
-            dma((9,)),
+            dma((5 + NSUB,)),
             dma((NCH, N)), dma((NCH, N)),
             dma((N,)), dma((N,)),
             dma((N,)), dma((N,)),
             dma((N,)), dma((N,)),
-            dma((N,)), dma((N,)),
-            dma((N,)), dma((N,)),
-            dma((NCH, N)), dma((NCH, N)),
+            dma((N,)), dma((3, SEG)),
+            dma((3, N)), dma((3, N)),
+            dma((2, SEG, NSUB)), dma((2, SEG, NSUB)),
+            dma((2, NSUB)), dma((NSUB,)),
             dma((N,)), dma((N,)),
             dma((N,)), dma((N,)),
         ],

time: 165 us -> 143 us (0.87)
  the two profiles are of different devices: /device:TPU:1 before, /device:TPU:4 now
where the time goes in v2:
time: 143 us
  Pallas kernels  135 us (94%)
  local copies, waits for them, and re-layouts  7 us (5%)
    pallas_call x1, Pallas kernels, per_device(): pl.pallas_call(kernel, out_shape=(jax.ShapeDtypeStruct((R, HID), bf16), j...  135 us
    unnamed x11, local copies, waits for them, and re-layouts  5.76 us

profile of v2, /device:TPU:4, one launch (start us, length us, event | category | flops | bytes accessed | tf_op | source)
XLA Modules:
  0.0 142.9 jit_solution(15218516698697519393)
XLA Ops:
  0.6 0.0 copy-start.2
  0.6 0.7 copy-done.2
  1.3 0.0 copy-start.3
  1.3 0.7 copy-done.3
  2.0 0.6 select_maximum_fusion.rm_ref
  2.6 134.6 %shard_map.93 = (bf16[384,1024]{1,0:T(8,128)(2,1)}, bf16[384,1024]{1,0:T(8,128)(2,1)}, f32[8,128]{1,0:T(8,128)}, bf16[1024,384]{1,0:T(8,128)(2,1)}) custom-call(bf16[128,384]{1,0:T(8,128)(2,1)} %x_ref.1, f32[8,128]{1,0:T(8,128)} %select_maximum_fusion.rm_ref, bf16[384,1024]{1,0:T(8,128)(2,1)} %bitcast.15, bf16[384,1024]{1,0:T(8,128)(2,1)} %bitcast.16, ...), custom_call_target="tpu_custom_call" | custom-call | flops 4831838208 | bytes 4718592 | tf_op jit(solution)/shard_map/pallas_call | solution.py:440
  137.2 1.2 slice_bitcast_fusion
  138.4 0.0 copy-start.1
  138.5 2.1 %copy.13 = bf16[1,1,8,48,1024]{4,3,2,1,0:T(8,128)(2,1)} copy(bf16[1,1,8,48,1024]{4,3,2,1,0:T(8,128)(2,1)} %bitcast.14) | data formatting | bytes 1572864
  140.6 0.0 copy-done.1
  140.6 0.0 copy-start
  140.6 0.9 copy.14
  141.5 0.5 copy-done
  142.0 0.9 copy.15
  (2 shorter events, 0.0 us)
Async XLA Ops:
  0.6 0.7 copy-start.2
  1.3 0.7 copy-start.3
  138.4 2.1 %copy-start.1 = (bf16[384,1024]{1,0:T(8,128)(2,1)S(1)}, bf16[384,1024]{1,0:T(8,128)(2,1)}, u32[]{:S(2)}) copy-start(bf16[384,1024]{1,0:T(8,128)(2,1)} %get-tuple-element.9) | copy-start | bytes 2359300
  140.6 1.4 copy-start

commit v3 on v2

v3 whole, which is shorter than its diff:
```python
import jax
import jax.numpy as jnp
from jax import lax
from jax.experimental import pallas as pl
from jax.experimental.pallas import tpu as pltpu
from jax.sharding import PartitionSpec as P

N = 8
CAP = 48
R = 384
HID = 1024
C = 384
CH = 256
NCH = 4
SUB = 128
NSUB = 8
SEG = 4
PLANE = (0, 1, 2, 3, 3, 3, 0, 0)
ROLE = (0, 0, 0, 0, 1, 2, 2, 1)
TOK = 128
MESH = pl.DeviceIdType.MESH


def copy_to(src, dst, send_sem, recv_sem, axis, index):
    return pltpu.make_async_remote_copy(
        src_ref=src,
        dst_ref=dst,
        send_sem=send_sem,
        recv_sem=recv_sem,
        device_id={axis: index},
        device_id_type=MESH,
    )


def kernel(
    x_ref, chosen_ref, share_ref, gate_hbm, up_hbm, w_hbm,
    gg_hbm, gu_hbm, gm_ref, down_hbm,
    wbuf, arows, abuf, xs, ms, mix, onehot, prow, weighted, a2buf, hbuf, hid, upstream, acc,
    gate, up, gg, gu, down, csend, crecv, psend, precv, rts, rtr, gms, gmr,
    io_sem, w_send, w_recv, a1_send, a1_recv, m_send, m_recv, f_send, f_recv,
    xd_send, xd_recv, xf_send, xf_recv, y_send, y_recv, g_send, g_recv, t_send, t_recv,
    a3_send, a3_recv, b_send, b_recv, a4_send, a4_recv, c_send, c_recv,
    h_send, h_recv, p_send, p_recv, r1_send, r1_recv, r2_send, r2_recv,
):
    z = lax.axis_index("dp")
    me = lax.axis_index("expert")
    h = lax.axis_index("etp")

    def peer(index, offset):
        return lax.rem(index + offset + N, N)

    pos = lax.rem(z + 2 * lax.rem(me, 2), SEG)
    start = peer(z, -pos)
    outer = (pos == 0) | (pos == SEG - 1)
    outward = jnp.where(pos < 2, -1, 1)
    hx = h // 2
    hy = lax.rem(h, 2)
    across = h + 1 - 2 * hy

    def along_x(i):
        return 2 * lax.rem(hx + i, 4) + hy

    barrier = pltpu.get_barrier_semaphore()
    for o in range(1, N):
        for axis, index in (("dp", z), ("expert", me), ("etp", h)):
            pl.semaphore_signal(
                barrier, inc=1, device_id={axis: peer(index, o)}, device_id_type=MESH
            )
    loads = [
        pltpu.make_async_copy(w_hbm, wbuf.at[pos], io_sem.at[0]),
        pltpu.make_async_copy(gate_hbm, gate, io_sem.at[1]),
        pltpu.make_async_copy(up_hbm, up, io_sem.at[2]),
    ]
    for load in loads:
        load.start()

    chosen_experts = chosen_ref[...].astype(jnp.float32)
    shares = share_ref[...].astype(jnp.float32)
    r0, r1 = chosen_experts[0:1, :], chosen_experts[1:2, :]
    m0, m1 = shares[0:1, :], shares[1:2, :]
    experts = lax.broadcasted_iota(jnp.int32, (N, TOK), 0).astype(jnp.float32)
    named = jnp.where((r0 == experts) | (r1 == experts), 1.0, 0.0)
    before = jnp.where(
        lax.broadcasted_iota(jnp.int32, (TOK, TOK), 0)
        < lax.broadcasted_iota(jnp.int32, (TOK, TOK), 1),
        1.0,
        0.0,
    ).astype(jnp.bfloat16)
    position = jnp.dot(named.astype(jnp.bfloat16), before, preferred_element_type=jnp.float32)
    place = lax.broadcasted_iota(jnp.int32, (CAP, TOK), 0).astype(jnp.float32)
    for e in range(N):
        chosen = jnp.where(
            (place == position[e : e + 1, :]) & (named[e : e + 1, :] > 0.0), 1.0, 0.0
        )
        onehot[e] = chosen
        weights = jnp.where(r0 == float(e), m0, 0.0) + jnp.where(r1 == float(e), m1, 0.0)
        column = jnp.sum(chosen * weights, axis=1, keepdims=True)
        ms[e] = jnp.broadcast_to(column, (CAP, TOK)).astype(jnp.bfloat16)
        xs[e] = jnp.dot(
            chosen.astype(jnp.bfloat16), x_ref[...], preferred_element_type=jnp.float32
        ).astype(jnp.bfloat16)

    loads[0].wait()
    pl.semaphore_wait(barrier, 3 * (N - 1))

    def along(bufs, step, part, way, arrival=False):
        buf, send, recv, size = bufs
        block = pos - way * (step + 1 if arrival else step)
        side = 0 if way > 0 else 1
        piece = buf.at[block, pl.ds(part * size, size)]
        return copy_to(
            piece, piece, send.at[side, step, part], recv.at[side, step, part], "dp", peer(z, way)
        )

    def sends(step, way):
        if way > 0:
            return (pos >= step) & (pos < SEG - 1)
        return (pos < SEG - step) & (pos > 0)

    def receives(step, way):
        return (pos > step) if way > 0 else (pos < SEG - 1 - step)

    def along_step(bufs, step, part):
        for way in (1, -1):
            if step > 0:

                @pl.when(receives(step - 1, way))
                def _(way=way):
                    along(bufs, step - 1, part, way, arrival=True).wait_recv()

            if step < SEG - 1:

                @pl.when(sends(step, way))
                def _(way=way):
                    along(bufs, step, part, way).start()

    def along_sent(bufs, parts):
        for way in (1, -1):
            for step in range(SEG - 1):

                @pl.when(sends(step, way))
                def _(way=way, step=step):
                    for part in range(parts):
                        along(bufs, step, part, way).wait_send()

    of_w = (wbuf, w_send, w_recv, CH)
    of_h = (hbuf, h_send, h_recv, SUB)

    along_step(of_w, 0, 0)
    along_step(of_w, 0, 1)

    def rows_of(index):
        return pl.ds(pl.multiple_of(index * CAP, CAP), CAP)

    def a1(o, arrival=False):
        dst = peer(me, o)
        where = rows_of(peer(me, -o) if arrival else me)
        return copy_to(xs.at[dst], arows.at[where], a1_send.at[o], a1_recv.at[o], "expert", dst)

    def m1(o, arrival=False):
        dst = peer(me, o)
        where = rows_of(peer(me, -o) if arrival else me)
        return copy_to(ms.at[dst], mix.at[where], m_send.at[o], m_recv.at[o], "expert", dst)

    for o in range(1, N):
        a1(o).start()
    for o in range(1, N):
        m1(o).start()
    arows[rows_of(me), :] = xs[me]
    mix[rows_of(me), :] = ms[me]

    along_step(of_w, 1, 0)
    for o in range(1, N):
        a1(o, arrival=True).wait_recv()

    def parts(o, arrival=False):
        dst = peer(h, o)
        slot = peer(peer(h, -o) if arrival else h, N - start)
        return copy_to(
            arows.at[rows_of(dst)], prow.at[slot], t_send.at[o], t_recv.at[o], "etp", dst
        )

    for o in range(1, N):
        parts(o).start()
    prow[peer(h, N - start)] = arows[rows_of(h), :]
    along_step(of_w, 0, 2)
    along_step(of_w, 1, 1)
    for o in range(1, N):
        parts(o, arrival=True).wait_recv()

    def abroad():
        role = jnp.where(outer, 1, 2)
        return copy_to(
            prow.at[pl.ds(SEG, SEG)],
            abuf.at[role, :, rows_of(h)],
            f_send.at[0],
            f_recv.at[role],
            "dp",
            peer(z, outward * role),
        )

    def own_x(i, arrival=False):
        where = rows_of(along_x(4 - i) if arrival else h)
        return copy_to(
            prow.at[pl.ds(0, SEG)],
            abuf.at[0, :, where],
            xd_send.at[i],
            xd_recv.at[i],
            "etp",
            along_x(i),
        )

    def own_y(i, arrival=False):
        place = along_x(4 - i)
        piece = abuf.at[0, :, rows_of(place + 1 - 2 * hy if arrival else place)]
        return copy_to(piece, piece, y_send.at[i], y_recv.at[i], "etp", across)

    def pair_y(buf, send, recv, role, arrival=False):
        piece = buf.at[role, :, rows_of(across if arrival else h)]
        return copy_to(piece, piece, send.at[role], recv.at[role], "etp", across)

    def pair_x(buf, send, recv, role, i, arrival=False):
        place = lax.rem(hx + (4 - i if arrival else 0), 4)
        piece = buf.at[role, :, pl.ds(pl.multiple_of(place * 2 * CAP, 2 * CAP), 2 * CAP)]
        return copy_to(
            piece, piece, send.at[role, i], recv.at[role, i], "etp", along_x(i)
        )

    def foreign_y(role, arrival=False):
        return pair_y(abuf, g_send, g_recv, role, arrival)

    def foreign_x(role, side, i, arrival=False):
        place = along_x(4 - i) if arrival else h
        piece = abuf.at[role, :, rows_of(place if side == 0 else place + 1 - 2 * hy)]
        return copy_to(
            piece, piece, xf_send.at[role, side, i], xf_recv.at[role, side, i], "etp", along_x(i)
        )

    abroad().start()
    for i in (2, 1, 3):
        own_x(i).start()
    abuf[0, :, rows_of(h), :] = prow[0:SEG]
    own_y(0).start()
    along_step(of_w, 0, 3)
    along_step(of_w, 1, 2)

    @pl.when(outer)
    def _():
        for role in (2, 1):
            piece = abuf.at[role, :, rows_of(h)]
            copy_to(piece, piece, f_send.at[0], f_recv.at[role], "dp", peer(z, 1)).wait_recv()
            foreign_y(role).start()
            for i in (2, 1, 3):
                foreign_x(role, 0, i).start()

    along_step(of_w, 2, 0)
    for i in (1, 3):
        own_x(i, arrival=True).wait_recv()
        own_y(i).start()

    @pl.when(outer)
    def _():
        for role in (2, 1):
            foreign_y(role, arrival=True).wait_recv()
            for i in (2, 1, 3):
                foreign_x(role, 1, i).start()

    along_step(of_w, 1, 3)
    own_x(2, arrival=True).wait_recv()
    own_y(2).start()
    along_step(of_w, 2, 1)
    for o in range(1, N):
        m1(o, arrival=True).wait_recv()
    share = mix[rows_of(h), 0:1].astype(jnp.float32)
    for o in range(N):
        weighted[o] = (share * prow[o].astype(jnp.float32)).astype(jnp.bfloat16)

    def a3(o):
        return copy_to(
            weighted.at[o],
            a2buf.at[ROLE[o], pos, rows_of(h)],
            a3_send.at[o],
            a3_recv.at[ROLE[o], pos],
            "dp",
            peer(start, PLANE[o]),
        )

    for o in range(N):

        @pl.when(pos != PLANE[o])
        def _(o=o):
            a3(o).start()

        @pl.when(pos == PLANE[o])
        def _(o=o):
            a2buf[ROLE[o], pos, rows_of(h), :] = weighted[o]

    along_step(of_w, 2, 2)
    along_step(of_w, 2, 3)
    for role in range(3):
        for block in range(SEG):

            @pl.when((pos != block) & ((role == 0) | outer))
            def _(role=role, block=block):
                piece = a2buf.at[role, block, rows_of(h)]
                copy_to(
                    piece, piece, a3_send.at[0], a3_recv.at[role, block], "dp", peer(start, block)
                ).wait_recv()

    def a4_y(role, arrival=False):
        return pair_y(a2buf, b_send, b_recv, role, arrival)

    def a4_x(role, i, arrival=False):
        return pair_x(a2buf, a4_send, a4_recv, role, i, arrival)

    def each_role(act):
        act(0)

        @pl.when(outer)
        def _():
            act(1)
            act(2)

    def each_a4_x(act):
        each_role(lambda role: [act(role, i) for i in (1, 2, 3)] and None)

    each_role(lambda role: a4_y(role).start())
    loads[1].wait()
    loads[2].wait()

    def product(role, chunk):
        total = None
        for block in range(SEG):
            term = lax.dot_general(
                abuf[role, block],
                wbuf[block, pl.ds(chunk * CH, CH), :],
                (((1,), (1,)), ((), ())),
                preferred_element_type=jnp.float32,
            )
            total = term if total is None else total + term
        return total

    def c_copy(role, chunk):
        return copy_to(
            csend.at[role - 1, chunk],
            crecv.at[chunk],
            c_send.at[role - 1, chunk],
            c_recv.at[chunk],
            "dp",
            peer(z, role * outward),
        )

    def multiply(role, chunk):
        if role == 0:
            upstream[chunk] = product(0, chunk)
            return

        @pl.when(outer)
        def _():
            csend[role - 1, chunk] = product(role, chunk).astype(jnp.bfloat16)
            c_copy(role, chunk).start()

    def foreign_here(role):
        @pl.when(outer)
        def _():
            for side in (0, 1):
                for i in (1, 2, 3):
                    foreign_x(role, side, i, arrival=True).wait_recv()

    RB = 64

    def terms_of(chunk):
        columns = pl.ds(chunk * CH, CH)

        def rows(i, carry):
            where = pl.ds(pl.multiple_of(i * RB, RB), RB)
            a = gate[where, columns].astype(jnp.float32)
            b = up[where, columns].astype(jnp.float32)
            u = upstream[chunk, where, :] + crecv[chunk, where, :].astype(jnp.float32)
            share = mix[where, 0:1].astype(jnp.float32)
            sig = jax.nn.sigmoid(a)
            silu = a * sig
            hidden = silu * b
            scaled = share * u
            gg[where, columns] = (scaled * b * sig * (1.0 + a * (1.0 - sig))).astype(jnp.bfloat16)
            gu[where, columns] = (scaled * silu).astype(jnp.bfloat16)
            hid[where, :] = hidden.astype(jnp.bfloat16)
            row_sum = jnp.broadcast_to(jnp.sum(u * hidden, axis=1, keepdims=True), (RB, TOK))
            if chunk == 0:
                rts[where, :] = row_sum
            else:
                rts[where, :] += row_sum
            return carry

        lax.fori_loop(0, R // RB, rows, 0)

    def activate(chunk):
        c_copy(1, chunk).wait_recv()
        terms_of(chunk)
        hbuf[pos, pl.ds(chunk * CH, CH), :] = hid[...].T
        for sub in subs(chunk):
            along_step(of_h, 0, sub)

    def grad(role, sub):
        total = None
        for block in range(SEG):
            term = jnp.dot(
                hbuf[block, pl.ds(sub * SUB, SUB), :],
                a2buf[role, block],
                preferred_element_type=jnp.float32,
            )
            total = term if total is None else total + term
        return total

    def partial(role, sub):
        return copy_to(
            psend.at[role - 1, pl.ds(sub * SUB, SUB)],
            precv.at[pl.ds(sub * SUB, SUB)],
            p_send.at[role - 1, sub],
            p_recv.at[sub],
            "dp",
            peer(z, role * outward),
        )

    def finish(sub):
        along_step(of_h, SEG - 1, sub)

        @pl.when(outer)
        def _():
            for role in (2, 1):
                psend[role - 1, pl.ds(sub * SUB, SUB), :] = grad(role, sub).astype(jnp.bfloat16)
                partial(role, sub).start()

        acc[sub] = grad(0, sub)

    def store_down(sub):
        where = pl.ds(sub * SUB, SUB)
        return pltpu.make_async_copy(down.at[where], down_hbm.at[where], io_sem.at[5 + sub])

    def conclude(sub):
        partial(1, sub).wait_recv()
        where = pl.ds(sub * SUB, SUB)
        down[where, :] = (acc[sub] + precv[where, :].astype(jnp.float32)).astype(jnp.bfloat16)
        store_down(sub).start()

    def subs(chunk):
        return (2 * chunk, 2 * chunk + 1)

    def r1_copy(o, arrival=False):
        dst = peer(me, o)
        slot = peer(me, -o) if arrival else me
        return copy_to(
            rts.at[rows_of(dst)], rtr.at[slot], r1_send.at[o], r1_recv.at[o], "expert", dst
        )

    def r2_copy(o, arrival=False):
        slot = peer(h, -o) if arrival else h
        return copy_to(gms, gmr.at[slot], r2_send.at[o], r2_recv.at[o], "etp", peer(h, o))

    stores = [
        pltpu.make_async_copy(gg, gg_hbm, io_sem.at[3]),
        pltpu.make_async_copy(gu, gu_hbm, io_sem.at[4]),
    ]
    for turn in range(NCH + 5):
        if turn == 0:
            along_step(of_w, SEG - 1, 0)
            along_step(of_w, SEG - 1, 1)
            foreign_here(2)
            multiply(2, 0)
            multiply(2, 1)
            for i in range(4):
                own_y(i, arrival=True).wait_recv()
            multiply(0, 0)
            foreign_here(1)
            multiply(1, 0)
            multiply(1, 1)
            multiply(0, 1)
        elif 2 <= turn < NCH:
            along_step(of_w, SEG - 1, turn)
            for role in (2, 1, 0):
                multiply(role, turn)
        if 0 <= turn - 1 < NCH:
            activate(turn - 1)
        for step in (1, 2):
            if 0 <= turn - 1 - step < NCH:
                for sub in subs(turn - 1 - step):
                    along_step(of_h, step, sub)
        if turn == 0:
            each_role(lambda role: a4_y(role, arrival=True).wait_recv())
            each_a4_x(lambda role, i: a4_x(role, i).start())
        if turn == 4:
            each_a4_x(lambda role, i: a4_x(role, i, arrival=True).wait_recv())
            for store in stores:
                store.start()
            for o in range(1, N):
                r1_copy(o).start()
            rtr[me] = rts[rows_of(me), :]
        if 0 <= turn - 4 < NCH:
            for sub in subs(turn - 4):
                finish(sub)
        if turn == 6:
            for o in range(1, N):
                r1_copy(o, arrival=True).wait_recv()
            gm0 = jnp.zeros((1, TOK), jnp.float32)
            gm1 = jnp.zeros((1, TOK), jnp.float32)
            for e in range(N):
                picked = jnp.sum(onehot[e] * rtr[e], axis=0, keepdims=True)
                gm0 += jnp.where(r0 == float(e), picked, 0.0)
                gm1 += jnp.where(r1 == float(e), picked, 0.0)
            row = lax.broadcasted_iota(jnp.int32, (N, TOK), 0)
            gms[...] = jnp.where(row == 0, gm0, jnp.where(row == 1, gm1, 0.0))
            for o in range(1, N):
                r2_copy(o).start()
            gmr[h] = gms[...]
        if 0 <= turn - 5 < NCH:
            for sub in subs(turn - 5):
                conclude(sub)
    for o in range(1, N):
        r2_copy(o, arrival=True).wait_recv()
    gm_ref[...] = jnp.sum(gmr[...], axis=0)[0:2, :]

    for store in stores:
        store.wait()
    for sub in range(NSUB):
        store_down(sub).wait()
    along_sent(of_w, NCH)
    along_sent(of_h, NSUB)

    @pl.when(outer)
    def _():
        for chunk in range(NCH):
            c_copy(1, chunk).wait_send()
            c_copy(2, chunk).wait_send()
        for sub in range(NSUB):
            partial(1, sub).wait_send()
            partial(2, sub).wait_send()

    abroad().wait_send()
    own_y(0).wait_send()
    for i in (1, 2, 3):
        own_x(i).wait_send()
        own_y(i).wait_send()

    @pl.when(outer)
    def _():
        for role in (1, 2):
            foreign_y(role).wait_send()
            for i in (1, 2, 3):
                foreign_x(role, 0, i).wait_send()
                foreign_x(role, 1, i).wait_send()

    for o in range(N):

        @pl.when(pos != PLANE[o])
        def _(o=o):
            a3(o).wait_send()

    each_role(lambda role: a4_y(role).wait_send())
    each_a4_x(lambda role, i: a4_x(role, i).wait_send())
    for o in range(1, N):
        a1(o).wait_send()
        m1(o).wait_send()
        parts(o).wait_send()
        r1_copy(o).wait_send()
        r2_copy(o).wait_send()


def per_device(grad_out, routing, mix_weights, gate_pre, up_pre, down_weight):
    vmem = pl.BlockSpec(memory_space=pltpu.VMEM)
    hbm = pl.BlockSpec(memory_space=pl.ANY)
    bf16, f32 = jnp.bfloat16, jnp.float32
    dma = pltpu.SemaphoreType.DMA
    gg, gu, gm, down = pl.pallas_call(
        kernel,
        out_shape=(
            jax.ShapeDtypeStruct((R, HID), bf16),
            jax.ShapeDtypeStruct((R, HID), bf16),
            jax.ShapeDtypeStruct((2, TOK), f32),
            jax.ShapeDtypeStruct((HID, C), bf16),
        ),
        in_specs=[vmem, vmem, vmem, hbm, hbm, hbm],
        out_specs=(hbm, hbm, vmem, hbm),
        scratch_shapes=[
            pltpu.VMEM((SEG, HID, C), bf16),
            pltpu.VMEM((R, C), bf16),
            pltpu.VMEM((3, SEG, R, C), bf16),
            pltpu.VMEM((N, CAP, C), bf16),
            pltpu.VMEM((N, CAP, TOK), bf16),
            pltpu.VMEM((R, TOK), bf16),
            pltpu.VMEM((N, CAP, TOK), f32),
            pltpu.VMEM((N, CAP, C), bf16),
            pltpu.VMEM((N, CAP, C), bf16),
            pltpu.VMEM((3, SEG, R, C), bf16),
            pltpu.VMEM((SEG, HID, R), bf16),
            pltpu.VMEM((R, CH), bf16),
            pltpu.VMEM((NCH, R, CH), f32),
            pltpu.VMEM((NSUB, SUB, C), f32),
            pltpu.VMEM((R, HID), bf16),
            pltpu.VMEM((R, HID), bf16),
            pltpu.VMEM((R, HID), bf16),
            pltpu.VMEM((R, HID), bf16),
            pltpu.VMEM((HID, C), bf16),
            pltpu.VMEM((2, NCH, R, CH), bf16),
            pltpu.VMEM((NCH, R, CH), bf16),
            pltpu.VMEM((2, HID, C), bf16),
            pltpu.VMEM((HID, C), bf16),
            pltpu.VMEM((R, TOK), f32),
            pltpu.VMEM((N, CAP, TOK), f32),
            pltpu.VMEM((N, TOK), f32),
            pltpu.VMEM((N, N, TOK), f32),
            dma((5 + NSUB,)),
            dma((2, SEG, NCH)), dma((2, SEG, NCH)),
            dma((N,)), dma((N,)),
            dma((N,)), dma((N,)),
            dma((1,)), dma((3,)),
            dma((4,)), dma((4,)),
            dma((3, 2, 4)), dma((3, 2, 4)),
            dma((4,)), dma((4,)),
            dma((3,)), dma((3,)),
            dma((N,)), dma((N,)),
            dma((N,)), dma((3, SEG)),
            dma((3,)), dma((3,)),
            dma((3, 4)), dma((3, 4)),
            dma((2, NCH)), dma((NCH,)),
            dma((2, SEG, NSUB)), dma((2, SEG, NSUB)),
            dma((2, NSUB)), dma((NSUB,)),
            dma((N,)), dma((N,)),
            dma((N,)), dma((N,)),
        ],
        compiler_params=pltpu.CompilerParams(
            collective_id=0, has_side_effects=True, vmem_limit_bytes=56 * 1024 * 1024
        ),
        cost_estimate=pl.CostEstimate(
            flops=4 * R * HID * C * N, bytes_accessed=6 * HID * C * 2, transcendentals=R * HID
        ),
    )(
        grad_out,
        routing.T,
        mix_weights.T,
        gate_pre.reshape(R, HID),
        up_pre.reshape(R, HID),
        down_weight.reshape(HID, C),
    )
    return (
        gg.reshape(gate_pre.shape),
        gu.reshape(gate_pre.shape),
        gm.T,
        down[None],
    )


def solution(mesh):
    in_specs = (
        P(("dp", "expert"), "etp"),
        P(("dp", "expert"), None),
        P(("dp", "expert"), None),
        P("dp", "expert", None, None, "etp"),
        P("dp", "expert", None, None, "etp"),
        P("expert", "etp", "dp"),
    )
    out_specs = (
        P("dp", "expert", None, None, "etp"),
        P("dp", "expert", None, None, "etp"),
        P(("dp", "expert"), None),
        P("expert", "etp", "dp"),
    )
    return jax.shard_map(
        per_device, mesh=mesh, in_specs=in_specs, out_specs=out_specs, check_vma=False
    )
```

time: 143 us -> 128 us (0.90)
  the two profiles are of different devices: /device:TPU:4 before, /device:TPU:14 now
where the time goes in v3:
time: 128 us
  Pallas kernels  123 us (96%)
  local copies, waits for them, and re-layouts  4.47 us (3%)
    pallas_call x1, Pallas kernels, per_device(): pl.pallas_call(kernel, out_shape=(jax.ShapeDtypeStruct((R, HID), bf16), j...  123 us
    unnamed x10, local copies, waits for them, and re-layouts  4.47 us

profile of v3, /device:TPU:14, one launch (start us, length us, event | category | flops | bytes accessed | tf_op | source)
XLA Modules:
  0.0 127.9 jit_solution(1199547315931335270)
XLA Ops:
  0.6 122.8 %shard_map.93 = (bf16[384,1024]{1,0:T(8,128)(2,1)}, bf16[384,1024]{1,0:T(8,128)(2,1)}, f32[2,128]{1,0:T(2,128)}, bf16[1024,384]{1,0:T(8,128)(2,1)}) custom-call(bf16[128,384]{1,0:T(8,128)(2,1)} %x_ref.1, s32[2,128]{1,0:T(2,128)} %bitcast.16, bf16[2,128]{1,0:T(2,128)(2,1)} %bitcast.17, bf16[384,1024]{1,0:T(8,128)(2,1)} %bitcast.13, ...), custom_call_target="tpu_custom_call" | custom-call | flops 4831838208 | bytes 4718592 | tf_op jit(solution)/shard_map/pallas_call | solution.py:573
  123.4 0.0 copy-start.1
  123.4 2.1 %copy.14 = bf16[1,1,8,48,1024]{4,3,2,1,0:T(8,128)(2,1)} copy(bf16[1,1,8,48,1024]{4,3,2,1,0:T(8,128)(2,1)} %bitcast.11) | data formatting | bytes 1572864
  125.6 0.0 copy-done.1
  125.6 0.0 copy-start.2
  125.6 0.0 copy-start
  125.6 0.9 copy.15
  126.5 0.0 copy-done.2
  126.5 0.6 copy.16
  127.0 0.0 copy-done
  127.0 0.9 copy.17
Async XLA Ops:
  123.4 2.1 %copy-start.1 = (bf16[384,1024]{1,0:T(8,128)(2,1)S(1)}, bf16[384,1024]{1,0:T(8,128)(2,1)}, u32[]{:S(2)}) copy-start(bf16[384,1024]{1,0:T(8,128)(2,1)} %get-tuple-element.9) | copy-start | bytes 2359300
  125.6 0.9 copy-start.2
  125.6 1.4 %copy-start = (bf16[1024,384]{1,0:T(8,128)(2,1)S(1)}, bf16[1024,384]{1,0:T(8,128)(2,1)}, u32[]{:S(2)}) copy-start(bf16[1024,384]{1,0:T(8,128)(2,1)} %get-tuple-element.11) | copy-start | bytes 2359300

commit v4 on v3

--- a/solution.py
+++ b/solution.py
@@ -12,13 +12,18 @@
 C = 384
 CH = 256
 NCH = 4
-SUB = 128
-NSUB = 8
 SEG = 4
-PLANE = (0, 1, 2, 3, 3, 3, 0, 0)
-ROLE = (0, 0, 0, 0, 1, 2, 2, 1)
 TOK = 128
 MESH = pl.DeviceIdType.MESH
+
+
+PLAN = (
+    "W0", "W1", "F2", "C20", "C21", "F1", "C10", "C11", "O", "C00",
+    "M", "W2", "C22", "C12", "A0", "C01", "W3", "C23", "C13", "A1",
+    "C02", "B0", "A2", "C03", "B1", "E0", "A3", "R", "B2", "E1",
+    "K0", "B3", "Z", "S", "E2", "K1", "D0", "E3", "K2", "D1",
+    "K3", "D2", "D3",
+)
 
 
 def copy_to(src, dst, send_sem, recv_sem, axis, index):
@@ -35,12 +40,11 @@
 def kernel(
     x_ref, chosen_ref, share_ref, gate_hbm, up_hbm, w_hbm,
     gg_hbm, gu_hbm, gm_ref, down_hbm,
-    wbuf, arows, abuf, xs, ms, mix, onehot, prow, weighted, a2buf, hbuf, hid, upstream, acc,
-    gate, up, gg, gu, down, csend, crecv, psend, precv, rts, rtr, gms, gmr,
+    wbuf, arows, abuf, xs, ms, mix, onehot, prow, hbuf, hid, upstream,
+    gate, up, gg, gu, down, csend, crecv, dsend, drecv, rts, rtr, gms, gmr,
     io_sem, w_send, w_recv, a1_send, a1_recv, m_send, m_recv, f_send, f_recv,
     xd_send, xd_recv, xf_send, xf_recv, y_send, y_recv, g_send, g_recv, t_send, t_recv,
-    a3_send, a3_recv, b_send, b_recv, a4_send, a4_recv, c_send, c_recv,
-    h_send, h_recv, p_send, p_recv, r1_send, r1_recv, r2_send, r2_recv,
+    c_send, c_recv, h_send, h_recv, d_send, d_recv, r1_send, r1_recv, r2_send, r2_recv,
 ):
     z = lax.axis_index("dp")
     me = lax.axis_index("expert")
@@ -53,6 +57,7 @@
     start = peer(z, -pos)
     outer = (pos == 0) | (pos == SEG - 1)
     outward = jnp.where(pos < 2, -1, 1)
+    inward = -outward
     hx = h // 2
     hy = lax.rem(h, 2)
     across = h + 1 - 2 * hy
@@ -144,7 +149,6 @@
                         along(bufs, step, part, way).wait_send()
 
     of_w = (wbuf, w_send, w_recv, CH)
-    of_h = (hbuf, h_send, h_recv, SUB)
 
     along_step(of_w, 0, 0)
     along_step(of_w, 0, 1)
@@ -215,19 +219,9 @@
         piece = abuf.at[0, :, rows_of(place + 1 - 2 * hy if arrival else place)]
         return copy_to(piece, piece, y_send.at[i], y_recv.at[i], "etp", across)
 
-    def pair_y(buf, send, recv, role, arrival=False):
-        piece = buf.at[role, :, rows_of(across if arrival else h)]
-        return copy_to(piece, piece, send.at[role], recv.at[role], "etp", across)
-
-    def pair_x(buf, send, recv, role, i, arrival=False):
-        place = lax.rem(hx + (4 - i if arrival else 0), 4)
-        piece = buf.at[role, :, pl.ds(pl.multiple_of(place * 2 * CAP, 2 * CAP), 2 * CAP)]
-        return copy_to(
-            piece, piece, send.at[role, i], recv.at[role, i], "etp", along_x(i)
-        )
-
     def foreign_y(role, arrival=False):
-        return pair_y(abuf, g_send, g_recv, role, arrival)
+        piece = abuf.at[role, :, rows_of(across if arrival else h)]
+        return copy_to(piece, piece, g_send.at[role], g_recv.at[role], "etp", across)
 
     def foreign_x(role, side, i, arrival=False):
         place = along_x(4 - i) if arrival else h
@@ -269,62 +263,8 @@
     own_x(2, arrival=True).wait_recv()
     own_y(2).start()
     along_step(of_w, 2, 1)
-    for o in range(1, N):
-        m1(o, arrival=True).wait_recv()
-    share = mix[rows_of(h), 0:1].astype(jnp.float32)
-    for o in range(N):
-        weighted[o] = (share * prow[o].astype(jnp.float32)).astype(jnp.bfloat16)
-
-    def a3(o):
-        return copy_to(
-            weighted.at[o],
-            a2buf.at[ROLE[o], pos, rows_of(h)],
-            a3_send.at[o],
-            a3_recv.at[ROLE[o], pos],
-            "dp",
-            peer(start, PLANE[o]),
-        )
-
-    for o in range(N):
-
-        @pl.when(pos != PLANE[o])
-        def _(o=o):
-            a3(o).start()
-
-        @pl.when(pos == PLANE[o])
-        def _(o=o):
-            a2buf[ROLE[o], pos, rows_of(h), :] = weighted[o]
-
     along_step(of_w, 2, 2)
     along_step(of_w, 2, 3)
-    for role in range(3):
-        for block in range(SEG):
-
-            @pl.when((pos != block) & ((role == 0) | outer))
-            def _(role=role, block=block):
-                piece = a2buf.at[role, block, rows_of(h)]
-                copy_to(
-                    piece, piece, a3_send.at[0], a3_recv.at[role, block], "dp", peer(start, block)
-                ).wait_recv()
-
-    def a4_y(role, arrival=False):
-        return pair_y(a2buf, b_send, b_recv, role, arrival)
-
-    def a4_x(role, i, arrival=False):
-        return pair_x(a2buf, a4_send, a4_recv, role, i, arrival)
-
-    def each_role(act):
-        act(0)
-
-        @pl.when(outer)
-        def _():
-            act(1)
-            act(2)
-
-    def each_a4_x(act):
-        each_role(lambda role: [act(role, i) for i in (1, 2, 3)] and None)
-
-    each_role(lambda role: a4_y(role).start())
     loads[1].wait()
     loads[2].wait()
 
@@ -384,7 +324,7 @@
             scaled = share * u
             gg[where, columns] = (scaled * b * sig * (1.0 + a * (1.0 - sig))).astype(jnp.bfloat16)
             gu[where, columns] = (scaled * silu).astype(jnp.bfloat16)
-            hid[where, :] = hidden.astype(jnp.bfloat16)
+            hid[where, :] = (share * hidden).astype(jnp.bfloat16)
             row_sum = jnp.broadcast_to(jnp.sum(u * hidden, axis=1, keepdims=True), (RB, TOK))
             if chunk == 0:
                 rts[where, :] = row_sum
@@ -397,54 +337,103 @@
     def activate(chunk):
         c_copy(1, chunk).wait_recv()
         terms_of(chunk)
-        hbuf[pos, pl.ds(chunk * CH, CH), :] = hid[...].T
-        for sub in subs(chunk):
-            along_step(of_h, 0, sub)
-
-    def grad(role, sub):
+        hbuf[0, pl.ds(chunk * CH, CH), :] = hid[...].T
+        hidden_abroad(chunk).start()
+
+    def hidden_abroad(chunk):
+        role = jnp.where(outer, 1, 2)
+        rows = pl.ds(chunk * CH, CH)
+        return copy_to(
+            hbuf.at[0, rows],
+            hbuf.at[role, rows],
+            h_send.at[chunk],
+            h_recv.at[role, chunk],
+            "dp",
+            peer(z, outward * role),
+        )
+
+    def hidden_here(role, chunk):
+        piece = hbuf.at[role, pl.ds(chunk * CH, CH)]
+        copy_to(piece, piece, h_send.at[chunk], h_recv.at[role, chunk], "dp", peer(z, 1)).wait_recv()
+
+    def grad(block, chunk, roles):
         total = None
-        for block in range(SEG):
+        for role in range(roles):
             term = jnp.dot(
-                hbuf[block, pl.ds(sub * SUB, SUB), :],
-                a2buf[role, block],
+                hbuf[role, pl.ds(chunk * CH, CH), :],
+                abuf[role, block],
                 preferred_element_type=jnp.float32,
             )
             total = term if total is None else total + term
         return total
 
-    def partial(role, sub):
-        return copy_to(
-            psend.at[role - 1, pl.ds(sub * SUB, SUB)],
-            precv.at[pl.ds(sub * SUB, SUB)],
-            p_send.at[role - 1, sub],
-            p_recv.at[sub],
+    w_in = jnp.where(inward > 0, 0, 1)
+    w_out = 1 - w_in
+
+    def sum_on(side, way, block, chunk):
+        rows = pl.ds(chunk * CH, CH)
+        return copy_to(
+            dsend.at[block, rows],
+            drecv.at[side, block, rows],
+            d_send.at[block, chunk],
+            d_recv.at[side, block, chunk],
             "dp",
-            peer(z, role * outward),
-        )
-
-    def finish(sub):
-        along_step(of_h, SEG - 1, sub)
-
+            peer(z, way),
+        )
+
+    def came(side, block, chunk):
+        sum_on(side, 1, block, chunk).wait_recv()
+        return drecv[side, block, pl.ds(chunk * CH, CH), :].astype(jnp.float32)
+
+    def sums_begin(chunk):
         @pl.when(outer)
         def _():
-            for role in (2, 1):
-                psend[role - 1, pl.ds(sub * SUB, SUB), :] = grad(role, sub).astype(jnp.bfloat16)
-                partial(role, sub).start()
-
-        acc[sub] = grad(0, sub)
-
-    def store_down(sub):
-        where = pl.ds(sub * SUB, SUB)
-        return pltpu.make_async_copy(down.at[where], down_hbm.at[where], io_sem.at[5 + sub])
-
-    def conclude(sub):
-        partial(1, sub).wait_recv()
-        where = pl.ds(sub * SUB, SUB)
-        down[where, :] = (acc[sub] + precv[where, :].astype(jnp.float32)).astype(jnp.bfloat16)
-        store_down(sub).start()
-
-    def subs(chunk):
-        return (2 * chunk, 2 * chunk + 1)
+            hidden_here(1, chunk)
+            hidden_here(2, chunk)
+            for far in (3, 2, 1):
+                block = pos + inward * far
+                dsend[block, pl.ds(chunk * CH, CH), :] = grad(block, chunk, 3).astype(jnp.bfloat16)
+                sum_on(w_in, inward, block, chunk).start()
+
+    def sums_inward(chunk):
+        @pl.when(jnp.logical_not(outer))
+        def _():
+            for far in (2, 1):
+                block = pos + inward * far
+                own = grad(block, chunk, 1)
+                dsend[block, pl.ds(chunk * CH, CH), :] = (
+                    own + came(w_in, block, chunk)
+                ).astype(jnp.bfloat16)
+                sum_on(w_in, inward, block, chunk).start()
+
+    def sums_outward(chunk):
+        @pl.when(jnp.logical_not(outer))
+        def _():
+            block = pos + outward
+            own = grad(block, chunk, 1)
+            dsend[block, pl.ds(chunk * CH, CH), :] = (
+                own + came(w_out, block, chunk)
+            ).astype(jnp.bfloat16)
+            sum_on(w_out, outward, block, chunk).start()
+
+    def store_down(chunk):
+        rows = pl.ds(chunk * CH, CH)
+        return pltpu.make_async_copy(down.at[rows], down_hbm.at[rows], io_sem.at[5 + chunk])
+
+    def conclude(chunk):
+        rows = pl.ds(chunk * CH, CH)
+
+        @pl.when(outer)
+        def _():
+            own = grad(pos, chunk, 3)
+            down[rows, :] = (own + came(w_out, pos, chunk)).astype(jnp.bfloat16)
+
+        @pl.when(jnp.logical_not(outer))
+        def _():
+            own = grad(pos, chunk, 1) + came(w_in, pos, chunk)
+            down[rows, :] = (own + came(w_out, pos, chunk)).astype(jnp.bfloat16)
+
+        store_down(chunk).start()
 
     def r1_copy(o, arrival=False):
         dst = peer(me, o)
@@ -461,108 +450,116 @@
         pltpu.make_async_copy(gg, gg_hbm, io_sem.at[3]),
         pltpu.make_async_copy(gu, gu_hbm, io_sem.at[4]),
     ]
-    for turn in range(NCH + 5):
-        if turn == 0:
-            along_step(of_w, SEG - 1, 0)
-            along_step(of_w, SEG - 1, 1)
-            foreign_here(2)
-            multiply(2, 0)
-            multiply(2, 1)
-            for i in range(4):
-                own_y(i, arrival=True).wait_recv()
-            multiply(0, 0)
-            foreign_here(1)
-            multiply(1, 0)
-            multiply(1, 1)
-            multiply(0, 1)
-        elif 2 <= turn < NCH:
-            along_step(of_w, SEG - 1, turn)
-            for role in (2, 1, 0):
-                multiply(role, turn)
-        if 0 <= turn - 1 < NCH:
-            activate(turn - 1)
-        for step in (1, 2):
-            if 0 <= turn - 1 - step < NCH:
-                for sub in subs(turn - 1 - step):
-                    along_step(of_h, step, sub)
-        if turn == 0:
-            each_role(lambda role: a4_y(role, arrival=True).wait_recv())
-            each_a4_x(lambda role, i: a4_x(role, i).start())
-        if turn == 4:
-            each_a4_x(lambda role, i: a4_x(role, i, arrival=True).wait_recv())
-            for store in stores:
-                store.start()
-            for o in range(1, N):
-                r1_copy(o).start()
-            rtr[me] = rts[rows_of(me), :]
-        if 0 <= turn - 4 < NCH:
-            for sub in subs(turn - 4):
-                finish(sub)
-        if turn == 6:
-            for o in range(1, N):
-                r1_copy(o, arrival=True).wait_recv()
-            gm0 = jnp.zeros((1, TOK), jnp.float32)
-            gm1 = jnp.zeros((1, TOK), jnp.float32)
-            for e in range(N):
-                picked = jnp.sum(onehot[e] * rtr[e], axis=0, keepdims=True)
-                gm0 += jnp.where(r0 == float(e), picked, 0.0)
-                gm1 += jnp.where(r1 == float(e), picked, 0.0)
-            row = lax.broadcasted_iota(jnp.int32, (N, TOK), 0)
-            gms[...] = jnp.where(row == 0, gm0, jnp.where(row == 1, gm1, 0.0))
-            for o in range(1, N):
-                r2_copy(o).start()
-            gmr[h] = gms[...]
-        if 0 <= turn - 5 < NCH:
-            for sub in subs(turn - 5):
-                conclude(sub)
+    def row_sums_out():
+        for store in stores:
+            store.start()
+        for o in range(1, N):
+            r1_copy(o).start()
+        rtr[me] = rts[rows_of(me), :]
+
+    def row_sums_picked():
+        for o in range(1, N):
+            r1_copy(o, arrival=True).wait_recv()
+        gm0 = jnp.zeros((1, TOK), jnp.float32)
+        gm1 = jnp.zeros((1, TOK), jnp.float32)
+        for e in range(N):
+            picked = jnp.sum(onehot[e] * rtr[e], axis=0, keepdims=True)
+            gm0 += jnp.where(r0 == float(e), picked, 0.0)
+            gm1 += jnp.where(r1 == float(e), picked, 0.0)
+        row = lax.broadcasted_iota(jnp.int32, (N, TOK), 0)
+        gms[...] = jnp.where(row == 0, gm0, jnp.where(row == 1, gm1, 0.0))
+        for o in range(1, N):
+            r2_copy(o).start()
+        gmr[h] = gms[...]
+
+    def own_here():
+        for i in range(4):
+            own_y(i, arrival=True).wait_recv()
+
+    def shares_here():
+        for o in range(1, N):
+            m1(o, arrival=True).wait_recv()
+
+    def early_sent():
+        along_sent(of_w, NCH)
+
+        @pl.when(outer)
+        def _():
+            for chunk in range(NCH):
+                c_copy(1, chunk).wait_send()
+                c_copy(2, chunk).wait_send()
+
+        abroad().wait_send()
+        own_y(0).wait_send()
+        for i in (1, 2, 3):
+            own_x(i).wait_send()
+            own_y(i).wait_send()
+
+        @pl.when(outer)
+        def _():
+            for role in (1, 2):
+                foreign_y(role).wait_send()
+                for i in (1, 2, 3):
+                    foreign_x(role, 0, i).wait_send()
+                    foreign_x(role, 1, i).wait_send()
+
+        for o in range(1, N):
+            a1(o).wait_send()
+            m1(o).wait_send()
+            parts(o).wait_send()
+
+    steps = dict(
+        W=lambda chunk: along_step(of_w, SEG - 1, chunk),
+        F=foreign_here,
+        O=own_here,
+        C=multiply,
+        A=activate,
+        B=sums_begin,
+        E=sums_inward,
+        K=sums_outward,
+        D=conclude,
+        M=shares_here,
+        R=row_sums_out,
+        S=row_sums_picked,
+        Z=early_sent,
+    )
+    for word in PLAN:
+        steps[word[0]](*[int(digit) for digit in word[1:]])
     for o in range(1, N):
         r2_copy(o, arrival=True).wait_recv()
     gm_ref[...] = jnp.sum(gmr[...], axis=0)[0:2, :]
 
     for store in stores:
         store.wait()
-    for sub in range(NSUB):
-        store_down(sub).wait()
-    along_sent(of_w, NCH)
-    along_sent(of_h, NSUB)
-
-    @pl.when(outer)
-    def _():
-        for chunk in range(NCH):
-            c_copy(1, chunk).wait_send()
-            c_copy(2, chunk).wait_send()
-        for sub in range(NSUB):
-            partial(1, sub).wait_send()
-            partial(2, sub).wait_send()
-
-    abroad().wait_send()
-    own_y(0).wait_send()
-    for i in (1, 2, 3):
-        own_x(i).wait_send()
-        own_y(i).wait_send()
-
-    @pl.when(outer)
-    def _():
-        for role in (1, 2):
-            foreign_y(role).wait_send()
-            for i in (1, 2, 3):
-                foreign_x(role, 0, i).wait_send()
-                foreign_x(role, 1, i).wait_send()
-
-    for o in range(N):
-
-        @pl.when(pos != PLANE[o])
-        def _(o=o):
-            a3(o).wait_send()
-
-    each_role(lambda role: a4_y(role).wait_send())
-    each_a4_x(lambda role, i: a4_x(role, i).wait_send())
-    for o in range(1, N):
-        a1(o).wait_send()
-        m1(o).wait_send()
-        parts(o).wait_send()
+    for chunk in range(NCH):
+        store_down(chunk).wait()
+        hidden_abroad(chunk).wait_send()
+        for o in range(1, SEG):
+            sum_on(w_in, 1, lax.rem(pos + o, SEG), chunk).wait_send()
+    for o in range(1, N):
         r1_copy(o).wait_send()
         r2_copy(o).wait_send()
+
+
+def hand_out(gg_in, gu_in, down_in, gm_in, gg_out, gu_out, down_out, gm_out, gg, gu, down, sem):
+    moves = []
+    for array, (src, mid, dst) in enumerate(
+        ((gg_in, gg, gg_out), (gu_in, gu, gu_out), (down_in, down, down_out))
+    ):
+        half = mid.shape[0] // 2
+        for part in range(2):
+            rows = pl.ds(part * half, half)
+            load = pltpu.make_async_copy(src.at[rows], mid.at[rows], sem.at[0, array, part])
+            load.start()
+            moves.append(
+                (load, pltpu.make_async_copy(mid.at[rows], dst.at[rows], sem.at[1, array, part]))
+            )
+    gm_out[...] = gm_in[...]
+    for load, store in moves:
+        load.wait()
+        store.start()
+    for load, store in moves:
+        store.wait()
 
 
 def per_device(grad_out, routing, mix_weights, gate_pre, up_pre, down_weight):
@@ -589,12 +586,9 @@
             pltpu.VMEM((R, TOK), bf16),
             pltpu.VMEM((N, CAP, TOK), f32),
             pltpu.VMEM((N, CAP, C), bf16),
-            pltpu.VMEM((N, CAP, C), bf16),
-            pltpu.VMEM((3, SEG, R, C), bf16),
-            pltpu.VMEM((SEG, HID, R), bf16),
+            pltpu.VMEM((3, HID, R), bf16),
             pltpu.VMEM((R, CH), bf16),
             pltpu.VMEM((NCH, R, CH), f32),
-            pltpu.VMEM((NSUB, SUB, C), f32),
             pltpu.VMEM((R, HID), bf16),
             pltpu.VMEM((R, HID), bf16),
             pltpu.VMEM((R, HID), bf16),
@@ -602,13 +596,13 @@
             pltpu.VMEM((HID, C), bf16),
             pltpu.VMEM((2, NCH, R, CH), bf16),
             pltpu.VMEM((NCH, R, CH), bf16),
-            pltpu.VMEM((2, HID, C), bf16),
-            pltpu.VMEM((HID, C), bf16),
+            pltpu.VMEM((SEG, HID, C), bf16),
+            pltpu.VMEM((2, SEG, HID, C), bf16),
             pltpu.VMEM((R, TOK), f32),
             pltpu.VMEM((N, CAP, TOK), f32),
             pltpu.VMEM((N, TOK), f32),
             pltpu.VMEM((N, N, TOK), f32),
-            dma((5 + NSUB,)),
+            dma((5 + NCH,)),
             dma((2, SEG, NCH)), dma((2, SEG, NCH)),
             dma((N,)), dma((N,)),
             dma((N,)), dma((N,)),
@@ -618,12 +612,9 @@
             dma((4,)), dma((4,)),
             dma((3,)), dma((3,)),
             dma((N,)), dma((N,)),
-            dma((N,)), dma((3, SEG)),
-            dma((3,)), dma((3,)),
-            dma((3, 4)), dma((3, 4)),
             dma((2, NCH)), dma((NCH,)),
-            dma((2, SEG, NSUB)), dma((2, SEG, NSUB)),
-            dma((2, NSUB)), dma((NSUB,)),
+            dma((NCH,)), dma((3, NCH)),
+            dma((SEG, NCH)), dma((2, SEG, NCH)),
             dma((N,)), dma((N,)),
             dma((N,)), dma((N,)),
         ],
@@ -641,6 +632,24 @@
         up_pre.reshape(R, HID),
         down_weight.reshape(HID, C),
     )
+    gg, gu, down, gm = pl.pallas_call(
+        hand_out,
+        out_shape=(
+            jax.ShapeDtypeStruct((R, HID), bf16),
+            jax.ShapeDtypeStruct((R, HID), bf16),
+            jax.ShapeDtypeStruct((HID, C), bf16),
+            jax.ShapeDtypeStruct((2, TOK), f32),
+        ),
+        in_specs=[hbm, hbm, hbm, vmem],
+        out_specs=(hbm, hbm, hbm, vmem),
+        scratch_shapes=[
+            pltpu.VMEM((R, HID), bf16),
+            pltpu.VMEM((R, HID), bf16),
+            pltpu.VMEM((HID, C), bf16),
+            dma((2, 3, 2)),
+        ],
+        compiler_params=pltpu.CompilerParams(vmem_limit_bytes=56 * 1024 * 1024),
+    )(gg, gu, down, gm)
     return (
         gg.reshape(gate_pre.shape),
         gu.reshape(gate_pre.shape),

time: 128 us -> 124 us (0.969)
  the two profiles are of different devices: /device:TPU:14 before, /device:TPU:1 now
where the time goes in v4:
time: 124 us; the launch traced here: 122 us
  Pallas kernels  121 us (98%)
    pallas_call x1, Pallas kernels, per_device(): pl.pallas_call(kernel, out_shape=(jax.ShapeDtypeStruct((R, HID), bf16), j...  117 us
    pallas_call x1, Pallas kernels, per_device(): pl.pallas_call(hand_out, out_shape=(jax.ShapeDtypeStruct((R, HID), bf16),...  3.73 us

profile of v4, /device:TPU:1, one launch (start us, length us, event | category | flops | bytes accessed | tf_op | source)
XLA Modules:
  0.0 121.8 jit_solution(6634328128289456736)
XLA Ops:
  0.6 117.2 %shard_map.93 = (bf16[384,1024]{1,0:T(8,128)(2,1)}, bf16[384,1024]{1,0:T(8,128)(2,1)}, f32[2,128]{1,0:T(2,128)}, bf16[1024,384]{1,0:T(8,128)(2,1)}) custom-call(bf16[128,384]{1,0:T(8,128)(2,1)} %x_ref.1, s32[2,128]{1,0:T(2,128)} %bitcast.15, bf16[2,128]{1,0:T(2,128)(2,1)} %bitcast.17, bf16[384,1024]{1,0:T(8,128)(2,1)} %bitcast.9, ...), custom_call_target="tpu_custom_call" | custom-call | flops 4831838208 | bytes 4718592 | tf_op jit(solution)/shard_map/pallas_call | solution.py:570
  117.9 3.7 %shard_map.94 = (bf16[384,1024]{1,0:T(8,128)(2,1)}, bf16[384,1024]{1,0:T(8,128)(2,1)}, bf16[1024,384]{1,0:T(8,128)(2,1)}, f32[2,128]{1,0:T(2,128)}) custom-call(bf16[384,1024]{1,0:T(8,128)(2,1)} %get-tuple-element.12.gg_in, bf16[384,1024]{1,0:T(8,128)(2,1)} %get-tuple-element.13.gu_in, bf16[1024,384]{1,0:T(8,128)(2,1)} %get-tuple-element.14.down_in, ...), custom_call_target="tpu_custom_call" | custom-call | tf_op jit(solution)/shard_map/pallas_call | solution.py:635

commit v5 on v4

--- a/solution.py
+++ b/solution.py
@@ -66,8 +66,10 @@
         return 2 * lax.rem(hx + i, 4) + hy
 
     barrier = pltpu.get_barrier_semaphore()
+    for o in (1, 2, N - 2, N - 1):
+        pl.semaphore_signal(barrier, inc=1, device_id={"dp": peer(z, o)}, device_id_type=MESH)
     for o in range(1, N):
-        for axis, index in (("dp", z), ("expert", me), ("etp", h)):
+        for axis, index in (("expert", me), ("etp", h)):
             pl.semaphore_signal(
                 barrier, inc=1, device_id={axis: peer(index, o)}, device_id_type=MESH
             )
@@ -106,7 +108,7 @@
         ).astype(jnp.bfloat16)
 
     loads[0].wait()
-    pl.semaphore_wait(barrier, 3 * (N - 1))
+    pl.semaphore_wait(barrier, 4 + 2 * (N - 1))
 
     def along(bufs, step, part, way, arrival=False):
         buf, send, recv, size = bufs
@@ -166,7 +168,7 @@
         where = rows_of(peer(me, -o) if arrival else me)
         return copy_to(ms.at[dst], mix.at[where], m_send.at[o], m_recv.at[o], "expert", dst)
 
-    for o in range(1, N):
+    for o in (4, 5, 3, 2, 6, 7, 1):
         a1(o).start()
     for o in range(1, N):
         m1(o).start()
@@ -184,7 +186,7 @@
             arows.at[rows_of(dst)], prow.at[slot], t_send.at[o], t_recv.at[o], "etp", dst
         )
 
-    for o in range(1, N):
+    for o in (4, 5, 3, 2, 6, 7, 1):
         parts(o).start()
     prow[peer(h, N - start)] = arows[rows_of(h), :]
     along_step(of_w, 0, 2)

time: 124 us -> 127 us (1.024)
  the two profiles are of different devices: /device:TPU:1 before, /device:TPU:266 now
where the time goes in v5:
time: 127 us
  Pallas kernels  126 us (99%)
    pallas_call x1, Pallas kernels, per_device(): pl.pallas_call(kernel, out_shape=(jax.ShapeDtypeStruct((R, HID), bf16), j...  122 us
    pallas_call x1, Pallas kernels, per_device(): pl.pallas_call(hand_out, out_shape=(jax.ShapeDtypeStruct((R, HID), bf16),...  3.73 us

profile of v5, /device:TPU:266, one launch (start us, length us, event | category | flops | bytes accessed | tf_op | source)
XLA Modules:
  0.0 126.9 jit_solution(3669796750167981249)
XLA Ops:
  0.6 122.3 %shard_map.93 = (bf16[384,1024]{1,0:T(8,128)(2,1)}, bf16[384,1024]{1,0:T(8,128)(2,1)}, f32[2,128]{1,0:T(2,128)}, bf16[1024,384]{1,0:T(8,128)(2,1)}) custom-call(bf16[128,384]{1,0:T(8,128)(2,1)} %x_ref.1, s32[2,128]{1,0:T(2,128)} %bitcast.15, bf16[2,128]{1,0:T(2,128)(2,1)} %bitcast.17, bf16[384,1024]{1,0:T(8,128)(2,1)} %bitcast.9, ...), custom_call_target="tpu_custom_call" | custom-call | flops 4831838208 | bytes 4718592 | tf_op jit(solution)/shard_map/pallas_call | solution.py:572
  123.0 3.7 %shard_map.94 = (bf16[384,1024]{1,0:T(8,128)(2,1)}, bf16[384,1024]{1,0:T(8,128)(2,1)}, bf16[1024,384]{1,0:T(8,128)(2,1)}, f32[2,128]{1,0:T(2,128)}) custom-call(bf16[384,1024]{1,0:T(8,128)(2,1)} %get-tuple-element.12.gg_in, bf16[384,1024]{1,0:T(8,128)(2,1)} %get-tuple-element.13.gu_in, bf16[1024,384]{1,0:T(8,128)(2,1)} %get-tuple-element.14.down_in, ...), custom_call_target="tpu_custom_call" | custom-call | tf_op jit(solution)/shard_map/pallas_call | solution.py:637
